TPU v7x, 128 devices: a whole 4x4x4 slice. The times are simulated.
128 devices in a mesh: sfc: 128 (over y, z, x, core).
Axes of the slice: x: 4, y: 4, z: 4, core: 2. Of those that a mesh axis runs over, the one named last changes fastest.
Arguments:
- state: float32 [5, 4, 4, 4, 65536], P(None, None, None, None, 'sfc'), may hold values from -6 to 6
- neighbour_map: int32 [6, 65536], P(None, 'sfc'), may hold values from 0 to 767, as said below
- layer_lists: int32 [2, 32768], P(None, 'sfc'), may hold values from 0 to 511, as said below
- forces: float32 [5, 65536], P(None, 'sfc'), may hold values from -24 to 24
- positions: float32 [3, 65536], P(None, 'sfc'), may hold values from -1 to 1
- route: int32 [65536, 1], P('sfc'), may hold values from 0 to 127; in each aligned block of 512 rows (0 to 511, 512 to 1023, ...) at most 8 rows name the same one
- element_slot: int32 [65536], P('sfc'), may hold values from 0 to 511
Outputs:
- new_state: float32 [5, 4, 4, 4, 65536], P(None, None, None, None, 'sfc')
Inputs may be any that keep to these rules, and one draw needn't show every extreme that they name: `neighbour_map`: each device's elements form a block of 16 x 16 x 2 elements, periodic in x and y, numbered in a drawn order; layer order is x fastest, then y. Faces along x and y name elements of the same device; -z faces of the bottom layer and +z faces of the top layer name 512 + the element's position in layer order, other z faces the element across on the same device. The connection is symmetric, devices in a loop along z. `layer_lists`: row 0 lists the bottom layer, row 1 the top layer of each device. `route`: among the points of one device, at most 8 name the same device.
All inputs are finite; a program needn't handle non-finite values.
Results may differ from a plain program's by a relative error of at most 0.0001.
Values sent between devices are 32-bit elements; how exact they have to be, the bound alone decides.
No kernel may reach another device: no remote copies, remote signals or barrier semaphores. Data moves between devices by JAX's collectives and lax.ppermute only.
A program may use at most 64 MiB of HBM per device.

v0:
```python
import functools

import jax
import jax.numpy as jnp
import numpy as np
from jax import lax
from jax.experimental import pallas as pl
from jax.experimental.pallas import tpu as pltpu
from jax.sharding import PartitionSpec as P

NODE_POINTS = (-1.0, -0.4472135954999579, 0.4472135954999579, 1.0)
GSCALE = 2.0
HALF_LIFT = 6.0
ADVECT = (0.6, -0.4, 0.8)
VISCOSITY = 0.02
TIME_STEP = 0.04

VARS = 5
CAP = 8
FIELDS = 9
GROUP = FIELDS * CAP
COLS = VARS * 4 * 2
TILES = COLS * 4
VMEM_LIMIT = 24 * 1024 * 1024
F32 = jnp.float32
BF16 = jnp.bfloat16


def diff_table():
    factor = [
        float(np.prod([NODE_POINTS[a] - NODE_POINTS[k] for k in range(4) if k != a]))
        for a in range(4)
    ]
    table = np.zeros((4, 4))
    for a in range(4):
        for b in range(4):
            if a != b:
                table[a, b] = factor[a] / factor[b] / (NODE_POINTS[a] - NODE_POINTS[b])
            else:
                table[a, b] = sum(
                    (1.0 / (NODE_POINTS[a] - NODE_POINTS[k]) for k in range(4) if k != a)
                )
    return table


SLOPE = GSCALE * diff_table()


def line_operator(direction):
    a, nu = ADVECT[direction], VISCOSITY
    out = np.zeros((4, 8))
    for col in range(8):
        value = np.zeros(8)
        value[col] = 1.0
        u, (um, gm, up, gp) = value[:4], value[4:]
        q = SLOPE @ u
        q[0] -= HALF_LIFT * (um - u[0])
        q[3] += HALF_LIFT * (up - u[3])
        qm = gm + HALF_LIFT * (u[0] - um)
        qp = gp - HALF_LIFT * (u[3] - up)
        res = -SLOPE @ (a * u - nu * q)
        for node, normal, ou, oq in ((0, -1.0, um, qm), (3, 1.0, up, qp)):
            along = normal * a
            res[node] += -HALF_LIFT * (along - abs(along)) * (ou - u[node])
            res[node] += HALF_LIFT * nu * normal * (oq - q[node])
        out[:, col] = res
    return out


LINES = [line_operator(d) for d in range(3)]
UM, GM, UP, GP = 4, 5, 6, 7


def rolled(x, shift):
    return pltpu.roll(x, shift % 8, 0)


def lanes(x, shift):
    return pltpu.roll(x, shift % 128, 1)


def combine(pairs):
    total = None
    for coef, value in pairs:
        if isinstance(coef, (float, np.floating)):
            if coef == 0.0:
                continue
            term = value if coef == 1.0 else value * float(coef)
        else:
            term = value * coef
        total = term if total is None else total + term
    return total


class Masks:
    def __init__(self):
        sub = lax.broadcasted_iota(jnp.int32, (8, 128), 0)
        lane = lax.broadcasted_iota(jnp.int32, (8, 128), 1)
        self.h0 = sub < 4
        self.l0 = (sub & 2) == 0
        self.r0 = (sub & 1) == 0
        self.x_first = (lane & 15) == 0
        self.x_last = (lane & 15) == 15
        self.y_wrap = (self.h0 & (lane < 16)) | (~self.h0 & (lane >= 112))
        self.sign = jnp.where(self.h0, 1.0, -1.0).astype(F32)

    def by_half(self, low, high):
        if low == high:
            return float(low)
        return jnp.where(self.h0, float(low), float(high)).astype(F32)


def transpose4(tiles, mk):
    v0, v1, v2, v3 = tiles
    x0 = jnp.where(mk.r0, v0, rolled(v1, 1))
    x1 = jnp.where(mk.r0, rolled(v0, -1), v1)
    x2 = jnp.where(mk.r0, v2, rolled(v3, 1))
    x3 = jnp.where(mk.r0, rolled(v2, -1), v3)
    w0 = jnp.where(mk.l0, x0, rolled(x2, 2))
    w2 = jnp.where(mk.l0, rolled(x0, -2), x2)
    w1 = jnp.where(mk.l0, x1, rolled(x3, 2))
    w3 = jnp.where(mk.l0, rolled(x1, -2), x3)
    return w0, w1, w2, w3


def rows8(index):
    return pl.ds(pl.multiple_of(index * 8, 8), 8)


def x_line(u, mk, mat):
    g0 = combine((SLOPE[0, b], u[b]) for b in range(4))
    g3 = combine((SLOPE[3, b], u[b]) for b in range(4))

    def before(t):
        return jnp.where(mk.x_first, lanes(t, -15), lanes(t, 1))

    def after(t):
        return jnp.where(mk.x_last, lanes(t, 15), lanes(t, -1))

    um, gm, up, gp = before(u[3]), before(g3), after(u[0]), after(g0)
    terms = list(u) + [um, gm, up, gp]
    return [combine((mat[a, c], terms[c]) for c in range(8)) for a in range(4)]


def y_coefs(mk, mat):
    out = []
    for jj in range(2):
        o = 3 - jj
        row = [mk.by_half(mat[jj, b], mat[o, 3 - b]) for b in range(4)]
        row.append(mk.by_half(mat[jj, UM], mat[o, UP]))
        row.append(mk.by_half(mat[jj, UP], mat[o, UM]))
        row.append(mk.by_half(mat[jj, GM], mat[o, GP]))
        out.append(row)
    return out


def y_line(u0, u1, mk, coefs):
    r0, r1 = rolled(u0, 4), rolled(u1, 4)
    g = combine(((SLOPE[0, 0], u0), (SLOPE[0, 1], u1), (SLOPE[0, 2], r1), (SLOPE[0, 3], r0)))
    g = rolled(g * mk.sign, 4)

    def outer(t):
        near = jnp.where(mk.h0, lanes(t, 16), lanes(t, -16))
        far = jnp.where(mk.r0, rolled(near, -1), rolled(near, 1))
        return jnp.where(mk.y_wrap, far, near)

    n, gn = outer(r0), outer(g)
    nr = rolled(n, 4)
    return [
        combine(zip(coefs[0], (u0, u1, r1, r0, n, nr, gn))),
        combine(zip(coefs[1][:6], (u0, u1, r1, r0, n, nr))),
    ]


def z_line(u, hu, hg, mk, mat):
    g0 = combine((SLOPE[0, b], u[b]) for b in range(4))
    g3 = combine((SLOPE[3, b], u[b]) for b in range(4))
    um = jnp.where(mk.l0, hu, rolled(u[3], 2))
    gm = jnp.where(mk.l0, hg, rolled(g3, 2))
    up = jnp.where(mk.l0, rolled(u[0], -2), hu)
    gp = jnp.where(mk.l0, rolled(g0, -2), hg)
    terms = list(u) + [um, gm, up, gp]
    return [combine((mat[a, c], terms[c]) for c in range(8)) for a in range(4)]


def apply_operator(src, dst, hu, hg, mk, scale, ident):
    mats = [scale * m for m in LINES]
    mats[2][:, :4] += ident * np.eye(4)
    coefs = y_coefs(mk, mats[1])

    def per_variable(v, carry):
        col = v * 8
        for c in range(8):
            u = [src[rows8((col + c) * 4 + k), :] for k in range(4)]
            new = z_line(u, hu[rows8(col + c), :], hg[rows8(col + c), :], mk, mats[2])
            for k in range(4):
                dst[rows8((col + c) * 4 + k), :] = new[k]
        for i in range(4):
            for k in range(4):
                at = [rows8((col + 2 * i + jj) * 4 + k) for jj in range(2)]
                new = y_line(src[at[0], :], src[at[1], :], mk, coefs)
                for jj in range(2):
                    dst[at[jj], :] += new[jj]
        for jj in range(2):
            for k in range(4):
                at = [rows8((col + 2 * i + jj) * 4 + k) for i in range(4)]
                new = x_line([src[a, :] for a in at], mk, mats[0])
                for i in range(4):
                    dst[at[i], :] += new[i]
        return carry

    lax.fori_loop(0, VARS, per_variable, 0)


def split2(x):
    hi = x.astype(BF16)
    return hi, (x - hi.astype(F32)).astype(BF16)


def nt_dot(a, b):
    return lax.dot_general(a, b, (((1,), (1,)), ((), ())), preferred_element_type=F32)


def fill_order(lists_ref, order):
    ids = lax.broadcasted_iota(jnp.int32, (512, 128), 0)
    for t in range(4):
        row = lists_ref[t // 2 : t // 2 + 1, (t % 2) * 128 : (t % 2) * 128 + 128]
        order[:, t * 128 : t * 128 + 128] = jnp.where(ids == row, 1.0, 0.0).astype(BF16)


def pack_points(route, payload, pack_ref):
    dest = lax.broadcasted_iota(jnp.int32, (128, 128), 0)
    lane = lax.broadcasted_iota(jnp.int32, (128, 128), 1)
    slot = lax.broadcasted_iota(jnp.int32, (8, 128), 0).astype(F32)
    to_device = [jnp.where(dest == route[:, t * 128 : t * 128 + 128], 1.0, 0.0) for t in range(4)]
    stacked = jnp.concatenate(to_device, axis=0).astype(BF16)
    before = jnp.where(dest < lane, 1.0, 0.0).astype(BF16)
    inside = jnp.dot(stacked, before, preferred_element_type=F32)
    totals = jnp.dot(stacked, jnp.ones((128, 128), BF16), preferred_element_type=F32)
    base = jnp.zeros((128, 128), F32)
    out = jnp.zeros((128, 128), F32)
    for t in range(4):
        here = slice(t * 128, t * 128 + 128)
        count = inside[here] + base
        base = base + totals[here]
        within = jnp.sum(count * to_device[t], axis=0, keepdims=True)
        chosen = slot == within
        rows = [jnp.where(chosen, p[:, here], 0.0) for p in payload]
        rows.append(jnp.zeros((128 - GROUP, 128), F32))
        rest = jnp.concatenate(rows, axis=0)
        for _ in range(3):
            part = rest.astype(BF16)
            rest = rest - part.astype(F32)
            out = out + nt_dot(stacked[here], part)
    low = pltpu.roll(pltpu.roll(out, 1, 0), GROUP, 1)
    up = pltpu.roll(pltpu.roll(out, 127, 0), 2 * GROUP - 128, 1)
    pack_ref[pl.ds(0, 128, stride=2), :] = jnp.where(lane < GROUP, out, low)
    pack_ref[pl.ds(1, 128, stride=2), :] = jnp.where(lane < 2 * GROUP - 128, low, up)


def entry_kernel(
    par_ref, route_ref, slot_ref, forces_ref, coords_ref, lists_ref, state_ref,
    pack_ref, u_ref, first_ref, second_ref, inv_ref, order, lhs,
):
    mk = Masks()
    payload = [forces_ref[f : f + 1, :] for f in range(5)]
    payload += [coords_ref[f : f + 1, :] for f in range(3)]
    payload.append(slot_ref[...].astype(F32))
    pack_points(route_ref[...], payload, pack_ref)

    fill_order(lists_ref, order)
    for vi in range(VARS * 4):
        x = jnp.concatenate([state_ref[vi * 4 + j] for j in (0, 3, 1, 2)], axis=0)
        hi, lo = split2(x)
        lhs[vi * 16 : vi * 16 + 16, :] = hi
        lhs[320 + vi * 16 : 336 + vi * 16, :] = lo
    res = jnp.dot(lhs[...], order[...], preferred_element_type=F32)
    val = res[:320] + res[320:]
    for g in range(COLS):
        tiles = [val[g * 8 : g * 8 + 8, t * 128 : t * 128 + 128] for t in range(4)]
        for k, tile in enumerate(transpose4(tiles, mk)):
            u_ref[(g * 4 + k) * 8 : (g * 4 + k) * 8 + 8, :] = tile

    place = lax.broadcasted_iota(jnp.int32, (16, 512), 1)
    digit = lax.broadcasted_iota(jnp.int32, (16, 512), 0)
    digits = jnp.where(digit == 0, place >> 4, place & 15).astype(F32).astype(BF16)
    where = nt_dot(digits, order[...])
    inv = where[0:1, :] * 16.0 + where[1:2, :]
    inv = jnp.concatenate([inv[:, t * 128 : t * 128 + 128] for t in range(4)] * 2, axis=0)
    inv_ref[...] = inv
    first_ref[2 * COLS * 8 :, :] = inv
    second_ref[2 * COLS * 8 :, :] = inv

    even = jnp.full((8, 128), par_ref[0], jnp.int32) == 0
    mat = TIME_STEP * LINES[2]
    top, bottom = np.eye(4)[3], np.eye(4)[0]

    def per_variable(v, carry):
        for c in range(8):
            col = v * 8 + c
            u = [u_ref[rows8(col * 4 + k), :] for k in range(4)]
            g0 = combine((SLOPE[0, b], u[b]) for b in range(4))
            g3 = combine((SLOPE[3, b], u[b]) for b in range(4))
            um, gm = rolled(u[3], 2), rolled(g3, 2)
            up, gp = rolled(u[0], -2), rolled(g0, -2)
            for part, (f_top, f_bottom, a_top, a_bottom) in enumerate(
                ((top, bottom, u[3], u[0]), (SLOPE[3], SLOPE[0], g3, g0))
            ):
                own = [u[0], u[1], u[2], u[3]]
                b_top = combine(
                    list(zip(f_top + f_top @ mat[:, :4], own))
                    + [(f_top @ mat[:, UM], um), (f_top @ mat[:, GM], gm)]
                )
                b_bottom = combine(
                    list(zip(f_bottom + f_bottom @ mat[:, :4], own))
                    + [(f_bottom @ mat[:, UP], up), (f_bottom @ mat[:, GP], gp)]
                )
                to_upper = jnp.where(mk.l0, rolled(a_top, -2), b_top)
                to_lower = jnp.where(mk.l0, b_bottom, rolled(a_bottom, 2))
                at = rows8(part * COLS + col)
                first_ref[at, :] = jnp.where(even, to_upper, to_lower)
                second_ref[at, :] = jnp.where(even, to_lower, to_upper)
        return carry

    lax.fori_loop(0, VARS, per_variable, 0)


def state_kernel(
    par_ref, u_ref, first_ref, second_ref, base_ref, au, ag, hu, hg, m0
):
    mk = Masks()
    even = jnp.full((8, 128), par_ref[0], jnp.int32) == 0
    mat = TIME_STEP * LINES[2]
    top, bottom = np.eye(4)[3], np.eye(4)[0]
    from_second = mk.l0 == even

    def unpack(col, carry):
        for part, (a, h) in enumerate(((au, hu), (ag, hg))):
            one = first_ref[rows8(part * COLS + col), :]
            two = second_ref[rows8(part * COLS + col), :]
            a[rows8(col), :] = jnp.where(from_second, two, one)
            rest = jnp.where(from_second, one, two)
            h[rows8(col), :] = jnp.where(mk.l0, rolled(rest, -2), rolled(rest, 2))
        return carry

    lax.fori_loop(0, COLS, unpack, 0, unroll=8)
    apply_operator(u_ref, m0, au, ag, mk, TIME_STEP, 1.0)

    x_mat, coefs = TIME_STEP * LINES[0], y_coefs(mk, TIME_STEP * LINES[1])

    def halo(v, carry):
        for c in range(8):
            col = v * 8 + c
            u = [u_ref[rows8(col * 4 + k), :] for k in range(4)]
            g0 = combine((SLOPE[0, b], u[b]) for b in range(4))
            g3 = combine((SLOPE[3, b], u[b]) for b in range(4))
            for h, f_low, f_high in ((hu, top, bottom), (hg, SLOPE[3], SLOPE[0])):
                low = combine(((f_low @ mat[:, UP], u[0]), (f_low @ mat[:, GP], g0)))
                high = combine(((f_high @ mat[:, UM], u[3]), (f_high @ mat[:, GM], g3)))
                h[rows8(col), :] += jnp.where(mk.l0, low, high)
        for a, h in ((au, hu), (ag, hg)):
            for i in range(4):
                at = [rows8(v * 8 + 2 * i + jj) for jj in range(2)]
                new = y_line(a[at[0], :], a[at[1], :], mk, coefs)
                for jj in range(2):
                    h[at[jj], :] += new[jj]
            for jj in range(2):
                at = [rows8(v * 8 + 2 * i + jj) for i in range(4)]
                new = x_line([a[r, :] for r in at], mk, x_mat)
                for i in range(4):
                    h[at[i], :] += new[i]
        return carry

    lax.fori_loop(0, VARS, halo, 0)
    apply_operator(m0, base_ref, hu, hg, mk, 0.5 * TIME_STEP, 0.5)

    def finish(n, carry):
        base_ref[rows8(n), :] += 0.5 * u_ref[rows8(n), :]
        return carry

    lax.fori_loop(0, TILES, finish, 0, unroll=16)


def line_basis(coords):
    rows = []
    for a in range(4):
        term = None
        for k in range(4):
            if k != a:
                factor = (coords - NODE_POINTS[k]) * (1.0 / (NODE_POINTS[a] - NODE_POINTS[k]))
                term = factor if term is None else term * factor
        rows.append(term)
    return rows


def place_of(slots, table, row):
    number = slots.astype(jnp.int32)
    inner, outer = number & 127, number >> 7
    found = jnp.zeros((8, 128), F32)
    for t in range(4):
        line = jnp.broadcast_to(table[row + t : row + t + 1, :], (8, 128))
        found = jnp.where(outer == t, jnp.take_along_axis(line, inner, axis=1), found)
    return found.astype(jnp.int32)


def source_kernel(
    par_ref, pts_ref, inv_ref, first_ref, second_ref, base_ref, lists_ref, out_ref,
    order, hot, hot_low, hot_up, lhs, lhs_low, lhs_up, grid, strength, su, sg, s_ref, new_ref,
):
    mk = Masks()
    even = jnp.full((8, 128), par_ref[0], jnp.int32) == 0
    halves = [pts_ref[pl.ds(h, 128, stride=2), :].T for h in range(2)]
    data = jnp.concatenate(halves, axis=0)
    tables = [
        inv_ref[...],
        jnp.where(even, second_ref[...], first_ref[...]),
        jnp.where(even, first_ref[...], second_ref[...]),
    ]
    ids = lax.broadcasted_iota(jnp.int32, (512, 128), 0)
    for group in range(3):
        field = [data[group * GROUP + f * 8 : group * GROUP + f * 8 + 8] for f in range(FIELDS)]
        forces = field[:5]
        bx, by, bz = [line_basis(field[5 + d]) for d in range(3)]
        place = place_of(field[8], tables[group], 0)
        if group == 0:
            columns = [forces[v] * bx[i] for v in range(VARS) for i in range(4)]
            nodes = [by[j] * bz[k] for j in (0, 3, 1, 2) for k in range(4)]
            goal, matrix, size, shift = hot, lhs, 512, 0
        else:
            node = 3 if group == 1 else 0
            slope = combine((SLOPE[node, b], bz[b]) for b in range(4))
            columns = [forces[v] * bz[node] for v in range(VARS)]
            columns += [forces[v] * slope for v in range(VARS)]
            nodes = [by[j] * bx[i] for j in (0, 3, 1, 2) for i in range(4)]
            goal, matrix, size = (hot_low, lhs_low, 256) if group == 1 else (hot_up, lhs_up, 256)
            shift = 256 if group == 1 else 0
        for n, tile in enumerate(nodes):
            grid[group, n * 8 : n * 8 + 8, :] = tile
        for n, tile in enumerate(columns):
            strength[group, n * 8 : n * 8 + 8, :] = tile
        count = len(columns) * 16
        for c in range(CAP):
            here = slice(c * 128, c * 128 + 128)
            node_rows = grid[group, pl.ds(c, 16, stride=8), :]
            for n in range(len(columns)):
                row = strength[group, n * 8 + c : n * 8 + c + 1, :]
                hi, lo = split2(node_rows * row)
                matrix[n * 16 : n * 16 + 16, here] = hi
                matrix[count + n * 16 : count + n * 16 + 16, here] = lo
            found = place[c : c + 1, :] - shift
            goal[:, here] = jnp.where(ids[:size] == found, 1.0, 0.0).astype(BF16)

    res = nt_dot(lhs[...], hot[...])
    val = res[:320] + res[320:]
    for g in range(COLS):
        tiles = [val[g * 8 : g * 8 + 8, t * 128 : t * 128 + 128] for t in range(4)]
        for k, tile in enumerate(transpose4(tiles, mk)):
            s_ref[(g * 4 + k) * 8 : (g * 4 + k) * 8 + 8, :] = tile
    res_low = nt_dot(lhs_low[...], hot_low[...])
    res_up = nt_dot(lhs_up[...], hot_up[...])
    val_low, val_up = res_low[:160] + res_low[160:], res_up[:160] + res_up[160:]
    for part, goal in ((0, su), (1, sg)):
        for v in range(VARS):
            for jj in range(2):
                at = (part * VARS + v) * 16 + jj * 8
                tiles = [
                    val[at : at + 8, t * 128 : t * 128 + 128]
                    for val in (val_low, val_up)
                    for t in range(2)
                ]
                for i, tile in enumerate(transpose4(tiles, mk)):
                    col = (v * 4 + i) * 2 + jj
                    goal[col * 8 : col * 8 + 8, :] = tile

    apply_operator(s_ref, new_ref, su, sg, mk, 0.5 * TIME_STEP * TIME_STEP, TIME_STEP)
    fill_order(lists_ref, order)
    for vi in range(VARS * 4):
        for jj in range(2):
            g = vi * 2 + jj
            at = [slice((g * 4 + k) * 8, (g * 4 + k) * 8 + 8) for k in range(4)]
            tiles = transpose4([new_ref[a, :] + base_ref[a, :] for a in at], mk)
            for t in range(4):
                new_ref[(g * 4 + t) * 8 : (g * 4 + t) * 8 + 8, :] = tiles[t]
        for t in range(4):
            x = jnp.concatenate(
                [new_ref[((vi * 2 + jj) * 4 + t) * 8 : ((vi * 2 + jj) * 4 + t) * 8 + 8, :] for jj in range(2)],
                axis=0,
            )
            hi, lo = split2(x)
            lhs[vi * 16 : vi * 16 + 16, t * 128 : t * 128 + 128] = hi
            lhs[320 + vi * 16 : 336 + vi * 16, t * 128 : t * 128 + 128] = lo
    res = nt_dot(lhs[:, :512], order[...])
    val = res[:320] + res[320:]
    for vi in range(VARS * 4):
        for n, j in enumerate((0, 3, 1, 2)):
            out_ref[vi * 4 + j] = val[vi * 16 + n * 4 : vi * 16 + n * 4 + 4, :]


def call(kernel, outs, scratch, specs):
    return pl.pallas_call(
        kernel,
        out_shape=outs,
        in_specs=specs,
        out_specs=jax.tree.map(lambda _: pl.BlockSpec(memory_space=pltpu.VMEM), outs),
        scratch_shapes=scratch,
        compiler_params=pltpu.CompilerParams(vmem_limit_bytes=VMEM_LIMIT),
    )


def tile_array(count):
    return jax.ShapeDtypeStruct((count * 8, 128), F32)


SMEM = pl.BlockSpec(memory_space=pltpu.SMEM)
VMEM = pl.BlockSpec(memory_space=pltpu.VMEM)


def entry_call(par, route, slots, forces, coords, lists, state):
    halo = tile_array(2 * COLS + 1)
    return call(
        entry_kernel,
        (jax.ShapeDtypeStruct((256, 128), F32), tile_array(TILES), halo, halo, tile_array(1)),
        [pltpu.VMEM((512, 512), BF16), pltpu.VMEM((640, 512), BF16)],
        [SMEM] + [VMEM] * 6,
    )(par, route, slots, forces, coords, lists, state)


def state_call(par, u, first, second):
    cols = pltpu.VMEM((COLS * 8, 128), F32)
    return call(
        state_kernel,
        tile_array(TILES),
        [cols, cols, cols, cols, pltpu.VMEM((TILES * 8, 128), F32)],
        [SMEM] + [VMEM] * 3,
    )(par, u, first, second)


def source_call(par, pts, inv, first, second, base, lists):
    cols = pltpu.VMEM((COLS * 8, 128), F32)
    field = pltpu.VMEM((TILES * 8, 128), F32)
    return call(
        source_kernel,
        jax.ShapeDtypeStruct((VARS * 16, 4, 512), F32),
        [
            pltpu.VMEM((512, 512), BF16),
            pltpu.VMEM((512, 1024), BF16),
            pltpu.VMEM((256, 1024), BF16),
            pltpu.VMEM((256, 1024), BF16),
            pltpu.VMEM((640, 1024), BF16),
            pltpu.VMEM((320, 1024), BF16),
            pltpu.VMEM((320, 1024), BF16),
            pltpu.VMEM((3, 128, 128), F32),
            pltpu.VMEM((3, 160, 128), F32),
            cols,
            cols,
            field,
            field,
        ],
        [SMEM] + [VMEM] * 6,
    )(par, pts, inv, first, second, base, lists)


def on_device(state, neighbour_map, layer_lists, forces, positions, route, element_slot):
    count = lax.axis_size("sfc")
    inside = [(d, d ^ 1) for d in range(count)]
    across = [(d, (d + 1) % count if d % 2 else (d - 1) % count) for d in range(count)]
    par = (lax.axis_index("sfc") & 1).astype(jnp.int32).reshape(1)
    pack, u, first, second, inv = entry_call(
        par,
        route.reshape(1, -1),
        element_slot.reshape(1, -1),
        forces,
        positions,
        layer_lists,
        state.reshape(VARS * 16, 4, -1),
    )
    first = lax.ppermute(first, "sfc", inside)
    second = lax.ppermute(second, "sfc", across)
    pts = lax.all_to_all(pack, "sfc", split_axis=0, concat_axis=0, tiled=True)
    base = state_call(par, u, first, second)
    tail = slice(2 * COLS * 8, None)
    out = source_call(par, pts, inv, first[tail], second[tail], base, layer_lists)
    return out.reshape(state.shape)


def solution(mesh):
    in_specs = (
        P(None, None, None, None, "sfc"),
        P(None, "sfc"),
        P(None, "sfc"),
        P(None, "sfc"),
        P(None, "sfc"),
        P("sfc", None),
        P("sfc"),
    )
    out_specs = P(None, None, None, None, "sfc")
    return jax.shard_map(
        on_device, mesh=mesh, in_specs=in_specs, out_specs=out_specs, check_vma=False
    )
```

profile of v0, /device:TPU:1, one launch (start us, length us, event | category | flops | bytes accessed | tf_op | source)
XLA Modules:
  0.0 33.3 jit_solution(13696306925495268766)
XLA Ops:
  0.0 0.0 copy-start.2
  0.0 0.0 copy-start.5
  0.0 0.0 copy-start.4
  0.0 0.0 copy-start.3
  0.0 0.7 %copy-done.2 = f32[3,512]{1,0:T(4,128)S(1)} copy-done((f32[3,512]{1,0:T(4,128)S(1)}, f32[3,512]{1,0:T(4,128)}, u32[]{:S(2)}) %copy-start.2) | copy-done | bytes 6168
  0.7 0.0 copy-done.5
  0.7 0.0 copy-done.4
  0.7 0.0 copy-done.3
  0.7 0.0 copy-start
  0.7 1.1 %copy-done = f32[5,4,4,4,512]{4,3,2,1,0:T(4,128)S(1)} copy-done((f32[5,4,4,4,512]{4,3,2,1,0:T(4,128)S(1)}, f32[5,4,4,4,512]{4,3,2,1,0:T(4,128)}, u32[]{:S(2)}) %copy-start) | copy-done | bytes 655384
  1.8 0.0 copy-start.1
  1.8 0.7 %copy-done.1 = f32[5,512]{1,0:T(8,128)S(1)} copy-done((f32[5,512]{1,0:T(8,128)S(1)}, f32[5,512]{1,0:T(8,128)}, u32[]{:S(2)}) %copy-start.1) | copy-done | bytes 10264
  2.5 2.1 %shard_map.64 = (f32[256,128]{1,0:T(8,128)}, f32[1280,128]{1,0:T(8,128)S(1)}, f32[648,128]{1,0:T(8,128)S(1)}, f32[648,128]{1,0:T(8,128)S(1)}, f32[8,128]{1,0:T(8,128)S(1)}) custom-call(s32[1]{0:T(128)} %bitcast.par_ref, s32[1,512]{1,0:T(1,128)S(1)} %bitcast.9, s32[1,512]{1,0:T(1,128)S(1)} %bitcast.10, f32[5,512]{1,0:T(8,128)S(1)} %copy-done.1, ...), custom_call_target="tpu_custom_call" | custom-call | tf_op jit(solution)/shard_map/pallas_call | solution.py:520
  4.6 1.4 %collective-permute-start = (f32[648,128]{1,0:T(8,128)S(1)}, f32[648,128]{1,0:T(8,128)S(1)}, u32[]{:S(2)}, u32[]{:S(2)}) collective-permute-start(f32[648,128]{1,0:T(8,128)S(1)} %get-tuple-element.12), channel_id=1, source_target_pairs={{0,1},{1,0},{2,3},{3,2},{4,5},{5,4},{6,7},{7,6},{8,9},{9,8},{10,11... | collective-permute-start | bytes 995336 | tf_op jit(solution)/shard_map/ppermute | solution.py:577
  6.0 1.2 %collective-permute-start.1 = (f32[648,128]{1,0:T(8,128)S(1)}, f32[648,128]{1,0:T(8,128)S(1)}, u32[]{:S(2)}, u32[]{:S(2)}) collective-permute-start(f32[648,128]{1,0:T(8,128)S(1)} %get-tuple-element.13), channel_id=1, source_target_pairs={{0,127},{1,2},{2,1},{3,4},{4,3},{5,6},{6,5},{7,8},{8,7},{9,10},{10... | collective-permute-start | bytes 995336 | tf_op jit(solution)/shard_map/ppermute | solution.py:578
  7.2 11.1 %all-to-all-start = ((f32[128,2,128]{2,1,0:T(2,128)}), f32[128,2,128]{2,1,0:T(2,128)S(1)}, u32[]{:S(2)}, u32[]{:S(2)}) async-start(f32[128,2,128]{2,1,0:T(2,128)} %bitcast.4), calls=%async_computation | async-start | bytes 262144 | tf_op jit(solution)/shard_map/all_to_all | solution.py:579
  18.3 0.0 collective-permute-done.first_ref
  18.4 0.0 collective-permute-done.1.second_ref
  18.4 3.5 %shard_map.65.base_ref = f32[1280,128]{1,0:T(8,128)S(1)} custom-call(s32[1]{0:T(128)} %bitcast.par_ref, f32[1280,128]{1,0:T(8,128)S(1)} %get-tuple-element.14.u_ref, f32[648,128]{1,0:T(8,128)S(1)} %collective-permute-done.first_ref, f32[648,128]{1,0:T(8,128)S(1)} %collective-permute-done.1.second_ref), custom_call_target="tpu_custom_call" | custom-call | tf_op jit(solution)/shard_map/pallas_call | solution.py:530
  21.9 6.5 %all-to-all-done = f32[128,2,128]{2,1,0:T(2,128)S(1)} async-done(((f32[128,2,128]{2,1,0:T(2,128)}), f32[128,2,128]{2,1,0:T(2,128)S(1)}, u32[]{:S(2)}, u32[]{:S(2)}) %all-to-all-start) | async-done | bytes 131104 | tf_op jit(solution)/shard_map/all_to_all | solution.py:579
  28.4 4.8 %shard_map.66 = f32[80,4,512]{2,1,0:T(4,128)} custom-call(s32[1]{0:T(128)} %bitcast.par_ref, f32[256,128]{1,0:T(8,128)S(1)} %bitcast.8, f32[8,128]{1,0:T(8,128)S(1)} %get-tuple-element.11.inv_ref, f32[8,128]{1,0:T(8,128)S(1)} %slice.8.first_ref, f32[8,128]{1,0:T(8,128)S(1)} %slice.9.second_ref, f32[1280,128]{1,0:T(8,128)S(1)} %shard_map.65.base_ref, ...), custom_call_target="tpu_custom_call" | custom-call | tf_op jit(solution)/shard_map/pallas_call | solution.py:541
  (2 shorter events, 0.0 us)
Async XLA Ops:
  0.0 0.7 %copy-start.2 = (f32[3,512]{1,0:T(4,128)S(1)}, f32[3,512]{1,0:T(4,128)}, u32[]{:S(2)}) copy-start(f32[3,512]{1,0:T(4,128)} %coords_ref.1) | copy-start | bytes 18436
  0.0 0.7 %copy-start.5 = (s32[512]{0:T(512)S(1)}, s32[512]{0:T(512)}, u32[]{:S(2)}) copy-start(s32[512]{0:T(512)} %param.12) | copy-start | bytes 6148
  0.0 0.7 %copy-start.4 = (s32[512,1]{0,1:T(1,128)S(1)}, s32[512,1]{0,1:T(1,128)}, u32[]{:S(2)}) copy-start(s32[512,1]{0,1:T(1,128)} %param.11) | copy-start | bytes 6148
  0.0 0.7 %copy-start.3 = (s32[2,256]{1,0:T(2,128)S(1)}, s32[2,256]{1,0:T(2,128)}, u32[]{:S(2)}) copy-start(s32[2,256]{1,0:T(2,128)} %lists_ref.3) | copy-start | bytes 6148
  0.7 1.1 %copy-start = (f32[5,4,4,4,512]{4,3,2,1,0:T(4,128)S(1)}, f32[5,4,4,4,512]{4,3,2,1,0:T(4,128)}, u32[]{:S(2)}) copy-start(f32[5,4,4,4,512]{4,3,2,1,0:T(4,128)} %param.7) | copy-start | bytes 1966084
  1.8 0.7 %copy-start.1 = (f32[5,512]{1,0:T(8,128)S(1)}, f32[5,512]{1,0:T(8,128)}, u32[]{:S(2)}) copy-start(f32[5,512]{1,0:T(8,128)} %forces_ref.1) | copy-start | bytes 30724
  4.6 13.7 %collective-permute-start = (f32[648,128]{1,0:T(8,128)S(1)}, f32[648,128]{1,0:T(8,128)S(1)}, u32[]{:S(2)}, u32[]{:S(2)}) collective-permute-start(f32[648,128]{1,0:T(8,128)S(1)} %get-tuple-element.12), channel_id=1, source_target_pairs={{0,1},{1,0},{2,3},{3,2},{4,5},{5,4},{6,7},{7,6},{8,9},{9,8},{10,11... | collective-permute-start | bytes 995336 | tf_op jit(solution)/shard_map/ppermute | solution.py:577
  6.0 12.3 %collective-permute-start.1 = (f32[648,128]{1,0:T(8,128)S(1)}, f32[648,128]{1,0:T(8,128)S(1)}, u32[]{:S(2)}, u32[]{:S(2)}) collective-permute-start(f32[648,128]{1,0:T(8,128)S(1)} %get-tuple-element.13), channel_id=1, source_target_pairs={{0,127},{1,2},{2,1},{3,4},{4,3},{5,6},{6,5},{7,8},{8,7},{9,10},{10... | collective-permute-start | bytes 995336 | tf_op jit(solution)/shard_map/ppermute | solution.py:578
  7.2 21.2 %all-to-all-start = ((f32[128,2,128]{2,1,0:T(2,128)}), f32[128,2,128]{2,1,0:T(2,128)S(1)}, u32[]{:S(2)}, u32[]{:S(2)}) async-start(f32[128,2,128]{2,1,0:T(2,128)} %bitcast.4), calls=%async_computation | async-start | bytes 262144 | tf_op jit(solution)/shard_map/all_to_all | solution.py:579
where the time goes:
time: 33.5 us; the launch traced here: 33.3 us
  starting transfers between devices  13.7 us (41%)
  Pallas kernels  10.4 us (31%)
  waiting for transfers between devices  6.53 us (19%)
  local copies, waits for them, and re-layouts  2.52 us (8%)
    all_to_all x1, starting transfers between devices, on_device(): pts = lax.all_to_all(pack, 'sfc', split_axis=0, concat_axis=0, tiled=True)  11.1 us
    all_to_all x1, waiting for transfers between devices, on_device(): pts = lax.all_to_all(pack, 'sfc', split_axis=0, concat_axis=0, tiled=True)  6.52 us
    pallas_call x1, Pallas kernels, source_call(): call(source_kernel, jax.ShapeDtypeStruct((VARS * 16, 4, 512), F32), [pltp...  4.81 us
    pallas_call x1, Pallas kernels, state_call(): call(state_kernel, tile_array(TILES), [cols, cols, cols, cols, pltpu.VMEM...  3.53 us
    unnamed x12, local copies, waits for them, and re-layouts  2.52 us
    pallas_call x1, Pallas kernels, entry_call(): call(entry_kernel, (jax.ShapeDtypeStruct((256, 128), F32), tile_array(TIL...  2.09 us
    ppermute x1, starting transfers between devices, on_device(): first = lax.ppermute(first, 'sfc', inside)  1.42 us
    ppermute x1, starting transfers between devices, on_device(): second = lax.ppermute(second, 'sfc', across)  1.18 us
  transfers between devices with their start and end apart: 3, of which 1 were waited for; matrix products, arithmetic and copies ran while one was open for 0% of the time, Pallas kernels for 11%

commit v1 on v0

--- a/solution.py
+++ b/solution.py
@@ -221,11 +221,10 @@
     return lax.dot_general(a, b, (((1,), (1,)), ((), ())), preferred_element_type=F32)
 
 
-def fill_order(lists_ref, order):
+def fill_order(rows, order):
     ids = lax.broadcasted_iota(jnp.int32, (512, 128), 0)
     for t in range(4):
-        row = lists_ref[t // 2 : t // 2 + 1, (t % 2) * 128 : (t % 2) * 128 + 128]
-        order[:, t * 128 : t * 128 + 128] = jnp.where(ids == row, 1.0, 0.0).astype(BF16)
+        order[:, t * 128 : t * 128 + 128] = jnp.where(ids == rows[t], 1.0, 0.0).astype(BF16)
 
 
 def pack_points(route, payload, pack_ref):
@@ -259,16 +258,30 @@
 
 
 def entry_kernel(
-    par_ref, route_ref, slot_ref, forces_ref, coords_ref, lists_ref, state_ref,
-    pack_ref, u_ref, first_ref, second_ref, inv_ref, order, lhs,
+    par_ref, route_hbm, slot_hbm, forces_hbm, coords_hbm, lists_hbm, state_hbm,
+    pack_ref, u_ref, first_ref, second_ref, inv_ref,
+    route_ref, slot_ref, forces_ref, coords_ref, lists_ref, state_ref, order, lhs, sems,
 ):
+    sources = (route_hbm, slot_hbm, forces_hbm, coords_hbm, lists_hbm, state_hbm)
+    targets = (route_ref, slot_ref, forces_ref, coords_ref, lists_ref, state_ref)
+    copies = [
+        pltpu.make_async_copy(a, b, sems.at[n]) for n, (a, b) in enumerate(zip(sources, targets))
+    ]
+    for copy in copies:
+        copy.start()
     mk = Masks()
+    for copy in copies[:5]:
+        copy.wait()
     payload = [forces_ref[f : f + 1, :] for f in range(5)]
     payload += [coords_ref[f : f + 1, :] for f in range(3)]
     payload.append(slot_ref[...].astype(F32))
     pack_points(route_ref[...], payload, pack_ref)
 
-    fill_order(lists_ref, order)
+    rows = [
+        lists_ref[t // 2 : t // 2 + 1, (t % 2) * 128 : (t % 2) * 128 + 128] for t in range(4)
+    ]
+    fill_order(rows, order)
+    copies[5].wait()
     for vi in range(VARS * 4):
         x = jnp.concatenate([state_ref[vi * 4 + j] for j in (0, 3, 1, 2)], axis=0)
         hi, lo = split2(x)
@@ -286,7 +299,8 @@
     digits = jnp.where(digit == 0, place >> 4, place & 15).astype(F32).astype(BF16)
     where = nt_dot(digits, order[...])
     inv = where[0:1, :] * 16.0 + where[1:2, :]
-    inv = jnp.concatenate([inv[:, t * 128 : t * 128 + 128] for t in range(4)] * 2, axis=0)
+    inv = [inv[:, t * 128 : t * 128 + 128] for t in range(4)]
+    inv = jnp.concatenate(inv + [row.astype(F32) for row in rows], axis=0)
     inv_ref[...] = inv
     first_ref[2 * COLS * 8 :, :] = inv
     second_ref[2 * COLS * 8 :, :] = inv
@@ -404,7 +418,7 @@
 
 
 def source_kernel(
-    par_ref, pts_ref, inv_ref, first_ref, second_ref, base_ref, lists_ref, out_ref,
+    par_ref, pts_ref, inv_ref, first_ref, second_ref, base_ref, out_ref,
     order, hot, hot_low, hot_up, lhs, lhs_low, lhs_up, grid, strength, su, sg, s_ref, new_ref,
 ):
     mk = Masks()
@@ -473,7 +487,7 @@
                     goal[col * 8 : col * 8 + 8, :] = tile
 
     apply_operator(s_ref, new_ref, su, sg, mk, 0.5 * TIME_STEP * TIME_STEP, TIME_STEP)
-    fill_order(lists_ref, order)
+    fill_order([inv_ref[4 + t : 5 + t, :].astype(jnp.int32) for t in range(4)], order)
     for vi in range(VARS * 4):
         for jj in range(2):
             g = vi * 2 + jj
@@ -517,12 +531,18 @@
 
 def entry_call(par, route, slots, forces, coords, lists, state):
     halo = tile_array(2 * COLS + 1)
+    arrays = (route, slots, forces, coords, lists, state)
     return call(
         entry_kernel,
         (jax.ShapeDtypeStruct((256, 128), F32), tile_array(TILES), halo, halo, tile_array(1)),
-        [pltpu.VMEM((512, 512), BF16), pltpu.VMEM((640, 512), BF16)],
-        [SMEM] + [VMEM] * 6,
-    )(par, route, slots, forces, coords, lists, state)
+        [pltpu.VMEM(x.shape, x.dtype) for x in arrays]
+        + [
+            pltpu.VMEM((512, 512), BF16),
+            pltpu.VMEM((640, 512), BF16),
+            pltpu.SemaphoreType.DMA((6,)),
+        ],
+        [SMEM] + [pl.BlockSpec(memory_space=pltpu.HBM)] * 6,
+    )(par, *[pltpu.with_memory_space_constraint(x, pltpu.HBM) for x in arrays])
 
 
 def state_call(par, u, first, second):
@@ -535,7 +555,7 @@
     )(par, u, first, second)
 
 
-def source_call(par, pts, inv, first, second, base, lists):
+def source_call(par, pts, inv, first, second, base):
     cols = pltpu.VMEM((COLS * 8, 128), F32)
     field = pltpu.VMEM((TILES * 8, 128), F32)
     return call(
@@ -556,8 +576,8 @@
             field,
             field,
         ],
-        [SMEM] + [VMEM] * 6,
-    )(par, pts, inv, first, second, base, lists)
+        [SMEM] + [VMEM] * 5,
+    )(par, pts, inv, first, second, base)
 
 
 def on_device(state, neighbour_map, layer_lists, forces, positions, route, element_slot):
@@ -574,12 +594,12 @@
         layer_lists,
         state.reshape(VARS * 16, 4, -1),
     )
+    second = lax.ppermute(second, "sfc", across)
     first = lax.ppermute(first, "sfc", inside)
-    second = lax.ppermute(second, "sfc", across)
     pts = lax.all_to_all(pack, "sfc", split_axis=0, concat_axis=0, tiled=True)
     base = state_call(par, u, first, second)
     tail = slice(2 * COLS * 8, None)
-    out = source_call(par, pts, inv, first[tail], second[tail], base, layer_lists)
+    out = source_call(par, pts, inv, first[tail], second[tail], base)
     return out.reshape(state.shape)
 
 

time: 33.5 us -> 32.3 us (0.964)
  local copies, waits for them, and re-layouts: 2.52 us -> 0.01 us
  Pallas kernels: 10.4 us -> 11.8 us
    unnamed x12 -> x0, local copies, waits for them, and re-layouts: 2.52 us -> none
    pallas_call x1, Pallas kernels: 2.09 us -> 3.44 us  [entry_call(): call(entry_kernel, (jax.ShapeDtypeStruct((256, 128), F32), tile_array(TIL...]
where the time goes in v1:
time: 32.3 us; the launch traced here: 32.2 us
  starting transfers between devices  13.8 us (43%)
  Pallas kernels  11.8 us (37%)
  waiting for transfers between devices  6.53 us (20%)
    all_to_all x1, starting transfers between devices, on_device(): pts = lax.all_to_all(pack, 'sfc', split_axis=0, concat_axis=0, tiled=True)  11 us
    all_to_all x1, waiting for transfers between devices, on_device(): pts = lax.all_to_all(pack, 'sfc', split_axis=0, concat_axis=0, tiled=True)  6.52 us
    pallas_call x1, Pallas kernels, source_call(): call(source_kernel, jax.ShapeDtypeStruct((VARS * 16, 4, 512), F32), [pltp...  4.82 us
    pallas_call x1, Pallas kernels, state_call(): call(state_kernel, tile_array(TILES), [cols, cols, cols, cols, pltpu.VMEM...  3.53 us
    pallas_call x1, Pallas kernels, entry_call(): call(entry_kernel, (jax.ShapeDtypeStruct((256, 128), F32), tile_array(TIL...  3.44 us
    ppermute x1, starting transfers between devices, on_device(): first = lax.ppermute(first, 'sfc', inside)  1.5 us
    ppermute x1, starting transfers between devices, on_device(): second = lax.ppermute(second, 'sfc', across)  1.27 us
  transfers between devices with their start and end apart: 3, of which 1 were waited for; matrix products, arithmetic and copies ran while one was open for 0% of the time, Pallas kernels for 11%

profile of v1, /device:TPU:1, one launch (start us, length us, event | category | flops | bytes accessed | tf_op | source)
XLA Modules:
  0.0 32.2 jit_solution(2676977024628938621)
XLA Ops:
  0.0 3.4 %shard_map.64 = (f32[256,128]{1,0:T(8,128)}, f32[1280,128]{1,0:T(8,128)S(1)}, f32[648,128]{1,0:T(8,128)S(1)}, f32[648,128]{1,0:T(8,128)S(1)}, f32[8,128]{1,0:T(8,128)S(1)}) custom-call(s32[1]{0:T(128)} %bitcast.par_ref, s32[1,512]{1,0:T(1,128)} %bitcast.9, s32[1,512]{1,0:T(1,128)} %bitcast.10, f32[5,512]{1,0:T(8,128)} %forces_hbm.1, f32[3,512]{1,0:T(4,128)} %coords_hbm.1, ...), custom_call_target="tpu_custom_call" | custom-call | tf_op jit(solution)/shard_map/pallas_call | solution.py:535
  3.5 1.5 %collective-permute-start = (f32[648,128]{1,0:T(8,128)S(1)}, f32[648,128]{1,0:T(8,128)S(1)}, u32[]{:S(2)}, u32[]{:S(2)}) collective-permute-start(f32[648,128]{1,0:T(8,128)S(1)} %get-tuple-element.12), channel_id=1, source_target_pairs={{0,1},{1,0},{2,3},{3,2},{4,5},{5,4},{6,7},{7,6},{8,9},{9,8},{10,11... | collective-permute-start | bytes 995336 | tf_op jit(solution)/shard_map/ppermute | solution.py:598
  5.0 1.3 %collective-permute-start.1 = (f32[648,128]{1,0:T(8,128)S(1)}, f32[648,128]{1,0:T(8,128)S(1)}, u32[]{:S(2)}, u32[]{:S(2)}) collective-permute-start(f32[648,128]{1,0:T(8,128)S(1)} %get-tuple-element.13), channel_id=1, source_target_pairs={{0,127},{1,2},{2,1},{3,4},{4,3},{5,6},{6,5},{7,8},{8,7},{9,10},{10... | collective-permute-start | bytes 995336 | tf_op jit(solution)/shard_map/ppermute | solution.py:597
  6.2 11.0 %all-to-all-start = ((f32[128,2,128]{2,1,0:T(2,128)}), f32[128,2,128]{2,1,0:T(2,128)S(1)}, u32[]{:S(2)}, u32[]{:S(2)}) async-start(f32[128,2,128]{2,1,0:T(2,128)} %bitcast.4), calls=%async_computation | async-start | bytes 262144 | tf_op jit(solution)/shard_map/all_to_all | solution.py:599
  17.2 0.0 collective-permute-done.first_ref
  17.3 0.0 collective-permute-done.1.second_ref
  17.3 3.5 %shard_map.65.base_ref = f32[1280,128]{1,0:T(8,128)S(1)} custom-call(s32[1]{0:T(128)} %bitcast.par_ref, f32[1280,128]{1,0:T(8,128)S(1)} %get-tuple-element.14.u_ref, f32[648,128]{1,0:T(8,128)S(1)} %collective-permute-done.first_ref, f32[648,128]{1,0:T(8,128)S(1)} %collective-permute-done.1.second_ref), custom_call_target="tpu_custom_call" | custom-call | tf_op jit(solution)/shard_map/pallas_call | solution.py:550
  20.8 6.5 %all-to-all-done = f32[128,2,128]{2,1,0:T(2,128)S(1)} async-done(((f32[128,2,128]{2,1,0:T(2,128)}), f32[128,2,128]{2,1,0:T(2,128)S(1)}, u32[]{:S(2)}, u32[]{:S(2)}) %all-to-all-start) | async-done | bytes 131104 | tf_op jit(solution)/shard_map/all_to_all | solution.py:599
  27.3 4.8 %shard_map.66 = f32[80,4,512]{2,1,0:T(4,128)} custom-call(s32[1]{0:T(128)} %bitcast.par_ref, f32[256,128]{1,0:T(8,128)S(1)} %bitcast.7, f32[8,128]{1,0:T(8,128)S(1)} %get-tuple-element.11.inv_ref, f32[8,128]{1,0:T(8,128)S(1)} %slice.8.first_ref, f32[8,128]{1,0:T(8,128)S(1)} %slice.9.second_ref, f32[1280,128]{1,0:T(8,128)S(1)} %shard_map.65.base_ref), custom_call_target="tpu_custom_call" | custom-call | tf_op jit(solution)/shard_map/pallas_call | solution.py:561
  (2 shorter events, 0.0 us)
Async XLA Ops:
  3.5 13.8 %collective-permute-start = (f32[648,128]{1,0:T(8,128)S(1)}, f32[648,128]{1,0:T(8,128)S(1)}, u32[]{:S(2)}, u32[]{:S(2)}) collective-permute-start(f32[648,128]{1,0:T(8,128)S(1)} %get-tuple-element.12), channel_id=1, source_target_pairs={{0,1},{1,0},{2,3},{3,2},{4,5},{5,4},{6,7},{7,6},{8,9},{9,8},{10,11... | collective-permute-start | bytes 995336 | tf_op jit(solution)/shard_map/ppermute | solution.py:598
  5.0 12.3 %collective-permute-start.1 = (f32[648,128]{1,0:T(8,128)S(1)}, f32[648,128]{1,0:T(8,128)S(1)}, u32[]{:S(2)}, u32[]{:S(2)}) collective-permute-start(f32[648,128]{1,0:T(8,128)S(1)} %get-tuple-element.13), channel_id=1, source_target_pairs={{0,127},{1,2},{2,1},{3,4},{4,3},{5,6},{6,5},{7,8},{8,7},{9,10},{10... | collective-permute-start | bytes 995336 | tf_op jit(solution)/shard_map/ppermute | solution.py:597
  6.2 21.1 %all-to-all-start = ((f32[128,2,128]{2,1,0:T(2,128)}), f32[128,2,128]{2,1,0:T(2,128)S(1)}, u32[]{:S(2)}, u32[]{:S(2)}) async-start(f32[128,2,128]{2,1,0:T(2,128)} %bitcast.4), calls=%async_computation | async-start | bytes 262144 | tf_op jit(solution)/shard_map/all_to_all | solution.py:599

commit v2 on v1

--- a/solution.py
+++ b/solution.py
@@ -110,20 +110,9 @@
         return jnp.where(self.h0, float(low), float(high)).astype(F32)
 
 
-def transpose4(tiles, mk):
-    v0, v1, v2, v3 = tiles
-    x0 = jnp.where(mk.r0, v0, rolled(v1, 1))
-    x1 = jnp.where(mk.r0, rolled(v0, -1), v1)
-    x2 = jnp.where(mk.r0, v2, rolled(v3, 1))
-    x3 = jnp.where(mk.r0, rolled(v2, -1), v3)
-    w0 = jnp.where(mk.l0, x0, rolled(x2, 2))
-    w2 = jnp.where(mk.l0, rolled(x0, -2), x2)
-    w1 = jnp.where(mk.l0, x1, rolled(x3, 2))
-    w3 = jnp.where(mk.l0, rolled(x1, -2), x3)
-    return w0, w1, w2, w3
-
-
 def rows8(index):
+    if isinstance(index, int):
+        return slice(index * 8, index * 8 + 8)
     return pl.ds(pl.multiple_of(index * 8, 8), 8)
 
 
@@ -183,12 +172,12 @@
     return [combine((mat[a, c], terms[c]) for c in range(8)) for a in range(4)]
 
 
-def apply_operator(src, dst, hu, hg, mk, scale, ident):
+def operator_of(src, dst, hu, hg, mk, scale, ident):
     mats = [scale * m for m in LINES]
     mats[2][:, :4] += ident * np.eye(4)
     coefs = y_coefs(mk, mats[1])
 
-    def per_variable(v, carry):
+    def per_variable(v):
         col = v * 8
         for c in range(8):
             u = [src[rows8((col + c) * 4 + k), :] for k in range(4)]
@@ -207,14 +196,39 @@
                 new = x_line([src[a, :] for a in at], mk, mats[0])
                 for i in range(4):
                     dst[at[i], :] += new[i]
+
+    return per_variable
+
+
+def apply_operator(*args):
+    one = operator_of(*args)
+
+    def body(v, carry):
+        one(v)
         return carry
 
-    lax.fori_loop(0, VARS, per_variable, 0)
+    lax.fori_loop(0, VARS, body, 0)
 
 
 def split2(x):
     hi = x.astype(BF16)
     return hi, (x - hi.astype(F32)).astype(BF16)
+
+
+def both(res):
+    half = res.shape[0] // 2
+    return res[:half] + res[half:]
+
+
+NODE_ROWS = (0, 1, 3, 2)
+
+
+def spread(val, goal, first):
+    for vi in range(val.shape[0] // 16):
+        for h in range(2):
+            for t in range(4):
+                tile = val[vi * 16 + h * 8 : vi * 16 + h * 8 + 8, t * 128 : t * 128 + 128]
+                goal[pl.ds((first + vi) * 64 + h * 4 + t, 8, stride=8), :] = tile
 
 
 def nt_dot(a, b):
@@ -257,10 +271,34 @@
     pack_ref[pl.ds(1, 128, stride=2), :] = jnp.where(lane < 2 * GROUP - 128, low, up)
 
 
+def fill_halo(u_ref, up_ref, down_ref, mk):
+    mat = TIME_STEP * LINES[2]
+    sides = ((3, 2, UM, GM, up_ref), (0, -2, UP, GP, down_ref))
+
+    def per_variable(v, carry):
+        for c in range(8):
+            col = v * 8 + c
+            u = [u_ref[rows8(col * 4 + k), :] for k in range(4)]
+            for node, shift, near, slope, goal in sides:
+                g = combine((SLOPE[node, b], u[b]) for b in range(4))
+                near_u, near_g = rolled(u[node], shift), rolled(g, shift)
+                for part, (row, a) in enumerate(((np.eye(4)[node], u[node]), (SLOPE[node], g))):
+                    b = combine(
+                        list(zip(row + row @ mat[:, :4], u))
+                        + [(row @ mat[:, near], near_u), (row @ mat[:, slope], near_g)]
+                    )
+                    a = rolled(a, -shift)
+                    tile = jnp.where(mk.l0, a, b) if node == 3 else jnp.where(mk.l0, b, a)
+                    goal[rows8(part * COLS + col), :] = tile
+        return carry
+
+    lax.fori_loop(0, VARS, per_variable, 0)
+
+
 def entry_kernel(
-    par_ref, route_hbm, slot_hbm, forces_hbm, coords_hbm, lists_hbm, state_hbm,
-    pack_ref, u_ref, first_ref, second_ref, inv_ref,
-    route_ref, slot_ref, forces_ref, coords_ref, lists_ref, state_ref, order, lhs, sems,
+    route_hbm, slot_hbm, forces_hbm, coords_hbm, lists_hbm, state_hbm,
+    pack_ref, u_ref, up_ref, down_ref, inv_ref, order,
+    route_ref, slot_ref, forces_ref, coords_ref, lists_ref, state_ref, lhs, sems,
 ):
     sources = (route_hbm, slot_hbm, forces_hbm, coords_hbm, lists_hbm, state_hbm)
     targets = (route_ref, slot_ref, forces_ref, coords_ref, lists_ref, state_ref)
@@ -283,16 +321,12 @@
     fill_order(rows, order)
     copies[5].wait()
     for vi in range(VARS * 4):
-        x = jnp.concatenate([state_ref[vi * 4 + j] for j in (0, 3, 1, 2)], axis=0)
+        x = jnp.concatenate([state_ref[vi * 4 + j] for j in NODE_ROWS], axis=0)
         hi, lo = split2(x)
         lhs[vi * 16 : vi * 16 + 16, :] = hi
         lhs[320 + vi * 16 : 336 + vi * 16, :] = lo
     res = jnp.dot(lhs[...], order[...], preferred_element_type=F32)
-    val = res[:320] + res[320:]
-    for g in range(COLS):
-        tiles = [val[g * 8 : g * 8 + 8, t * 128 : t * 128 + 128] for t in range(4)]
-        for k, tile in enumerate(transpose4(tiles, mk)):
-            u_ref[(g * 4 + k) * 8 : (g * 4 + k) * 8 + 8, :] = tile
+    spread(both(res), u_ref, 0)
 
     place = lax.broadcasted_iota(jnp.int32, (16, 512), 1)
     digit = lax.broadcasted_iota(jnp.int32, (16, 512), 0)
@@ -300,61 +334,25 @@
     where = nt_dot(digits, order[...])
     inv = where[0:1, :] * 16.0 + where[1:2, :]
     inv = [inv[:, t * 128 : t * 128 + 128] for t in range(4)]
-    inv = jnp.concatenate(inv + [row.astype(F32) for row in rows], axis=0)
+    inv = jnp.concatenate(inv + inv, axis=0)
     inv_ref[...] = inv
-    first_ref[2 * COLS * 8 :, :] = inv
-    second_ref[2 * COLS * 8 :, :] = inv
-
-    even = jnp.full((8, 128), par_ref[0], jnp.int32) == 0
+    up_ref[2 * COLS * 8 :, :] = inv
+    down_ref[2 * COLS * 8 :, :] = inv
+
+    fill_halo(u_ref, up_ref, down_ref, mk)
+
+
+def state_kernel(u_ref, before_ref, after_ref, base_ref, au, ag, hu, hg, m0):
+    mk = Masks()
     mat = TIME_STEP * LINES[2]
     top, bottom = np.eye(4)[3], np.eye(4)[0]
 
-    def per_variable(v, carry):
-        for c in range(8):
-            col = v * 8 + c
-            u = [u_ref[rows8(col * 4 + k), :] for k in range(4)]
-            g0 = combine((SLOPE[0, b], u[b]) for b in range(4))
-            g3 = combine((SLOPE[3, b], u[b]) for b in range(4))
-            um, gm = rolled(u[3], 2), rolled(g3, 2)
-            up, gp = rolled(u[0], -2), rolled(g0, -2)
-            for part, (f_top, f_bottom, a_top, a_bottom) in enumerate(
-                ((top, bottom, u[3], u[0]), (SLOPE[3], SLOPE[0], g3, g0))
-            ):
-                own = [u[0], u[1], u[2], u[3]]
-                b_top = combine(
-                    list(zip(f_top + f_top @ mat[:, :4], own))
-                    + [(f_top @ mat[:, UM], um), (f_top @ mat[:, GM], gm)]
-                )
-                b_bottom = combine(
-                    list(zip(f_bottom + f_bottom @ mat[:, :4], own))
-                    + [(f_bottom @ mat[:, UP], up), (f_bottom @ mat[:, GP], gp)]
-                )
-                to_upper = jnp.where(mk.l0, rolled(a_top, -2), b_top)
-                to_lower = jnp.where(mk.l0, b_bottom, rolled(a_bottom, 2))
-                at = rows8(part * COLS + col)
-                first_ref[at, :] = jnp.where(even, to_upper, to_lower)
-                second_ref[at, :] = jnp.where(even, to_lower, to_upper)
-        return carry
-
-    lax.fori_loop(0, VARS, per_variable, 0)
-
-
-def state_kernel(
-    par_ref, u_ref, first_ref, second_ref, base_ref, au, ag, hu, hg, m0
-):
-    mk = Masks()
-    even = jnp.full((8, 128), par_ref[0], jnp.int32) == 0
-    mat = TIME_STEP * LINES[2]
-    top, bottom = np.eye(4)[3], np.eye(4)[0]
-    from_second = mk.l0 == even
-
     def unpack(col, carry):
         for part, (a, h) in enumerate(((au, hu), (ag, hg))):
-            one = first_ref[rows8(part * COLS + col), :]
-            two = second_ref[rows8(part * COLS + col), :]
-            a[rows8(col), :] = jnp.where(from_second, two, one)
-            rest = jnp.where(from_second, one, two)
-            h[rows8(col), :] = jnp.where(mk.l0, rolled(rest, -2), rolled(rest, 2))
+            low = before_ref[rows8(part * COLS + col), :]
+            high = after_ref[rows8(part * COLS + col), :]
+            a[rows8(col), :] = jnp.where(mk.l0, low, high)
+            h[rows8(col), :] = jnp.where(mk.l0, rolled(low, -2), rolled(high, 2))
         return carry
 
     lax.fori_loop(0, COLS, unpack, 0, unroll=8)
@@ -417,105 +415,124 @@
     return found.astype(jnp.int32)
 
 
-def source_kernel(
-    par_ref, pts_ref, inv_ref, first_ref, second_ref, base_ref, out_ref,
-    order, hot, hot_low, hot_up, lhs, lhs_low, lhs_up, grid, strength, su, sg, s_ref, new_ref,
-):
-    mk = Masks()
-    even = jnp.full((8, 128), par_ref[0], jnp.int32) == 0
-    halves = [pts_ref[pl.ds(h, 128, stride=2), :].T for h in range(2)]
-    data = jnp.concatenate(halves, axis=0)
-    tables = [
-        inv_ref[...],
-        jnp.where(even, second_ref[...], first_ref[...]),
-        jnp.where(even, first_ref[...], second_ref[...]),
-    ]
-    ids = lax.broadcasted_iota(jnp.int32, (512, 128), 0)
-    for group in range(3):
-        field = [data[group * GROUP + f * 8 : group * GROUP + f * 8 + 8] for f in range(FIELDS)]
-        forces = field[:5]
-        bx, by, bz = [line_basis(field[5 + d]) for d in range(3)]
-        place = place_of(field[8], tables[group], 0)
-        if group == 0:
-            columns = [forces[v] * bx[i] for v in range(VARS) for i in range(4)]
-            nodes = [by[j] * bz[k] for j in (0, 3, 1, 2) for k in range(4)]
-            goal, matrix, size, shift = hot, lhs, 512, 0
-        else:
-            node = 3 if group == 1 else 0
-            slope = combine((SLOPE[node, b], bz[b]) for b in range(4))
-            columns = [forces[v] * bz[node] for v in range(VARS)]
-            columns += [forces[v] * slope for v in range(VARS)]
-            nodes = [by[j] * bx[i] for j in (0, 3, 1, 2) for i in range(4)]
-            goal, matrix, size = (hot_low, lhs_low, 256) if group == 1 else (hot_up, lhs_up, 256)
-            shift = 256 if group == 1 else 0
+def fill_hots(hots, places):
+    ids = lax.broadcasted_iota(jnp.int32, (16, 128), 0)
+    places = [[jnp.broadcast_to(p[c : c + 1, :], (16, 128)) for c in range(CAP)] for p in places]
+
+    def body(n, carry):
+        for hot, place in zip(hots, places):
+            count = hot.shape[0] // 256
+            for m in range(count):
+                first = (n * count + m) * 16
+                here = ids + first
+                for c in range(CAP):
+                    at = pl.ds(pl.multiple_of(first, 16), 16)
+                    hot[at, c * 128 : c * 128 + 128] = jnp.where(here == place[c], 1.0, 0.0).astype(BF16)
+        return carry
+
+    lax.fori_loop(0, 16, body, 0)
+
+
+def fill_terms(matrix, columns, nodes, strength, grid, group, first, count):
+    if first == 0:
         for n, tile in enumerate(nodes):
             grid[group, n * 8 : n * 8 + 8, :] = tile
         for n, tile in enumerate(columns):
             strength[group, n * 8 : n * 8 + 8, :] = tile
-        count = len(columns) * 16
-        for c in range(CAP):
-            here = slice(c * 128, c * 128 + 128)
-            node_rows = grid[group, pl.ds(c, 16, stride=8), :]
-            for n in range(len(columns)):
-                row = strength[group, n * 8 + c : n * 8 + c + 1, :]
-                hi, lo = split2(node_rows * row)
-                matrix[n * 16 : n * 16 + 16, here] = hi
-                matrix[count + n * 16 : count + n * 16 + 16, here] = lo
-            found = place[c : c + 1, :] - shift
-            goal[:, here] = jnp.where(ids[:size] == found, 1.0, 0.0).astype(BF16)
-
-    res = nt_dot(lhs[...], hot[...])
-    val = res[:320] + res[320:]
-    for g in range(COLS):
-        tiles = [val[g * 8 : g * 8 + 8, t * 128 : t * 128 + 128] for t in range(4)]
-        for k, tile in enumerate(transpose4(tiles, mk)):
-            s_ref[(g * 4 + k) * 8 : (g * 4 + k) * 8 + 8, :] = tile
-    res_low = nt_dot(lhs_low[...], hot_low[...])
-    res_up = nt_dot(lhs_up[...], hot_up[...])
-    val_low, val_up = res_low[:160] + res_low[160:], res_up[:160] + res_up[160:]
+    for c in range(CAP):
+        here = slice(c * 128, c * 128 + 128)
+        node_rows = grid[group, pl.ds(c, 16, stride=8), :]
+        for n in range(first, first + count):
+            hi, lo = split2(node_rows * strength[group, n * 8 + c : n * 8 + c + 1, :])
+            at = (first + n) * 16
+            matrix[at : at + 16, here] = hi
+            matrix[at + count * 16 : at + count * 16 + 16, here] = lo
+
+
+def trace_terms(field, node):
+    bx, by, bz = [line_basis(field[5 + d]) for d in range(3)]
+    slope = combine((SLOPE[node, b], bz[b]) for b in range(4))
+    columns = [field[v] * bz[node] for v in range(VARS)]
+    columns += [field[v] * slope for v in range(VARS)]
+    pairs = [(i, j) for h in range(2) for i in range(4) for j in NODE_ROWS[2 * h : 2 * h + 2]]
+    return columns, [by[j] * bx[i] for i, j in pairs]
+
+
+SPANS = ((0, 3), (3, 2))
+
+
+def source_kernel(
+    pts_ref, inv_ref, before_ref, after_ref, base_ref, order, out_hbm,
+    hot, hot_low, hot_up, lhs, lhs_low, lhs_up, grid, strength, su, sg, s_ref, new_ref,
+    lhs_out, out_ref, sems,
+):
+    mk = Masks()
+    halves = [pts_ref[pl.ds(h, 128, stride=2), :].T for h in range(2)]
+    data = jnp.concatenate(halves, axis=0)
+    field = [
+        [data[g * GROUP + f * 8 : g * GROUP + f * 8 + 8] for f in range(FIELDS)] for g in range(3)
+    ]
+    fill_hots(
+        (hot_low, hot_up, hot),
+        (
+            place_of(field[1][8], before_ref, 0) - 256,
+            place_of(field[2][8], after_ref, 0),
+            place_of(field[0][8], inv_ref, 0),
+        ),
+    )
+    traces = []
+    for group, node, matrix, goal in ((1, 3, lhs_low, hot_low), (2, 0, lhs_up, hot_up)):
+        fill_terms(matrix, *trace_terms(field[group], node), strength, grid, group, 0, 10)
+        traces.append(both(nt_dot(matrix[...], goal[...])))
+    bx, by, bz = [line_basis(field[0][5 + d]) for d in range(3)]
+    columns = [field[0][v] * bx[i] for v in range(VARS) for i in range(4)]
+    nodes = [by[j] * bz[k] for j in NODE_ROWS for k in range(4)]
+    vals = []
+    for first, count in SPANS:
+        fill_terms(lhs, columns, nodes, strength, grid, 0, first * 4, count * 4)
+        vals.append(both(nt_dot(lhs[first * 128 : (first + count) * 128, :], hot[...])))
     for part, goal in ((0, su), (1, sg)):
         for v in range(VARS):
-            for jj in range(2):
-                at = (part * VARS + v) * 16 + jj * 8
-                tiles = [
-                    val[at : at + 8, t * 128 : t * 128 + 128]
-                    for val in (val_low, val_up)
-                    for t in range(2)
-                ]
-                for i, tile in enumerate(transpose4(tiles, mk)):
-                    col = (v * 4 + i) * 2 + jj
-                    goal[col * 8 : col * 8 + 8, :] = tile
-
-    apply_operator(s_ref, new_ref, su, sg, mk, 0.5 * TIME_STEP * TIME_STEP, TIME_STEP)
-    fill_order([inv_ref[4 + t : 5 + t, :].astype(jnp.int32) for t in range(4)], order)
-    for vi in range(VARS * 4):
-        for jj in range(2):
-            g = vi * 2 + jj
-            at = [slice((g * 4 + k) * 8, (g * 4 + k) * 8 + 8) for k in range(4)]
-            tiles = transpose4([new_ref[a, :] + base_ref[a, :] for a in at], mk)
+            for h in range(2):
+                at = (part * VARS + v) * 16 + h * 8
+                for t in range(4):
+                    tile = traces[t // 2][at : at + 8, (t % 2) * 128 : (t % 2) * 128 + 128]
+                    goal[pl.ds(v * 64 + h * 4 + t, 8, stride=8), :] = tile
+
+    one = operator_of(s_ref, new_ref, su, sg, mk, 0.5 * TIME_STEP * TIME_STEP, TIME_STEP)
+    for (first, count), val in zip(SPANS, vals):
+        spread(val, s_ref, first * 4)
+        for v in range(first, first + count):
+            one(v)
+    copies = []
+    for n, (first, count) in enumerate(SPANS):
+        for vi in range(first * 4, (first + count) * 4):
+            at = (first * 4 + vi) * 16
             for t in range(4):
-                new_ref[(g * 4 + t) * 8 : (g * 4 + t) * 8 + 8, :] = tiles[t]
-        for t in range(4):
-            x = jnp.concatenate(
-                [new_ref[((vi * 2 + jj) * 4 + t) * 8 : ((vi * 2 + jj) * 4 + t) * 8 + 8, :] for jj in range(2)],
-                axis=0,
-            )
-            hi, lo = split2(x)
-            lhs[vi * 16 : vi * 16 + 16, t * 128 : t * 128 + 128] = hi
-            lhs[320 + vi * 16 : 336 + vi * 16, t * 128 : t * 128 + 128] = lo
-    res = nt_dot(lhs[:, :512], order[...])
-    val = res[:320] + res[320:]
-    for vi in range(VARS * 4):
-        for n, j in enumerate((0, 3, 1, 2)):
-            out_ref[vi * 4 + j] = val[vi * 16 + n * 4 : vi * 16 + n * 4 + 4, :]
-
-
-def call(kernel, outs, scratch, specs):
+                rows = [pl.ds(vi * 64 + h * 4 + t, 8, stride=8) for h in range(2)]
+                x = jnp.concatenate([new_ref[r, :] + base_ref[r, :] for r in rows], axis=0)
+                hi, lo = split2(x)
+                lhs_out[at : at + 16, t * 128 : t * 128 + 128] = hi
+                at_lo = at + count * 64
+                lhs_out[at_lo : at_lo + 16, t * 128 : t * 128 + 128] = lo
+        val = both(nt_dot(lhs_out[first * 128 : (first + count) * 128, :], order[...]))
+        for vi in range(first * 4, (first + count) * 4):
+            for m, j in enumerate(NODE_ROWS):
+                at = (vi - first * 4) * 16 + m * 4
+                out_ref[vi * 4 + j] = val[at : at + 4, :]
+        part = pl.ds(first * 16, count * 16)
+        copies.append(pltpu.make_async_copy(out_ref.at[part], out_hbm.at[part], sems.at[n]))
+        copies[-1].start()
+    for copy in copies:
+        copy.wait()
+
+
+def call(kernel, outs, scratch, specs, place=pltpu.VMEM):
     return pl.pallas_call(
         kernel,
         out_shape=outs,
         in_specs=specs,
-        out_specs=jax.tree.map(lambda _: pl.BlockSpec(memory_space=pltpu.VMEM), outs),
+        out_specs=jax.tree.map(lambda _: pl.BlockSpec(memory_space=place), outs),
         scratch_shapes=scratch,
         compiler_params=pltpu.CompilerParams(vmem_limit_bytes=VMEM_LIMIT),
     )
@@ -525,44 +542,47 @@
     return jax.ShapeDtypeStruct((count * 8, 128), F32)
 
 
-SMEM = pl.BlockSpec(memory_space=pltpu.SMEM)
 VMEM = pl.BlockSpec(memory_space=pltpu.VMEM)
 
 
-def entry_call(par, route, slots, forces, coords, lists, state):
-    halo = tile_array(2 * COLS + 1)
+def entry_call(route, slots, forces, coords, lists, state):
     arrays = (route, slots, forces, coords, lists, state)
     return call(
         entry_kernel,
-        (jax.ShapeDtypeStruct((256, 128), F32), tile_array(TILES), halo, halo, tile_array(1)),
+        (
+            jax.ShapeDtypeStruct((256, 128), F32),
+            tile_array(TILES),
+            tile_array(2 * COLS + 1),
+            tile_array(2 * COLS + 1),
+            tile_array(1),
+            jax.ShapeDtypeStruct((512, 512), BF16),
+        ),
         [pltpu.VMEM(x.shape, x.dtype) for x in arrays]
         + [
-            pltpu.VMEM((512, 512), BF16),
             pltpu.VMEM((640, 512), BF16),
             pltpu.SemaphoreType.DMA((6,)),
         ],
-        [SMEM] + [pl.BlockSpec(memory_space=pltpu.HBM)] * 6,
-    )(par, *[pltpu.with_memory_space_constraint(x, pltpu.HBM) for x in arrays])
-
-
-def state_call(par, u, first, second):
+        [pl.BlockSpec(memory_space=pltpu.HBM)] * 6,
+    )(*[pltpu.with_memory_space_constraint(x, pltpu.HBM) for x in arrays])
+
+
+def state_call(u, before, after):
     cols = pltpu.VMEM((COLS * 8, 128), F32)
     return call(
         state_kernel,
         tile_array(TILES),
         [cols, cols, cols, cols, pltpu.VMEM((TILES * 8, 128), F32)],
-        [SMEM] + [VMEM] * 3,
-    )(par, u, first, second)
-
-
-def source_call(par, pts, inv, first, second, base):
+        [VMEM] * 3,
+    )(u, before, after)
+
+
+def source_call(pts, inv, before, after, base, order):
     cols = pltpu.VMEM((COLS * 8, 128), F32)
     field = pltpu.VMEM((TILES * 8, 128), F32)
     return call(
         source_kernel,
         jax.ShapeDtypeStruct((VARS * 16, 4, 512), F32),
         [
-            pltpu.VMEM((512, 512), BF16),
             pltpu.VMEM((512, 1024), BF16),
             pltpu.VMEM((256, 1024), BF16),
             pltpu.VMEM((256, 1024), BF16),
@@ -575,18 +595,20 @@
             cols,
             field,
             field,
+            pltpu.VMEM((640, 512), BF16),
+            pltpu.VMEM((VARS * 16, 4, 512), F32),
+            pltpu.SemaphoreType.DMA((2,)),
         ],
-        [SMEM] + [VMEM] * 5,
-    )(par, pts, inv, first, second, base)
+        [VMEM] * 6,
+        pltpu.HBM,
+    )(pts, inv, before, after, base, order)
 
 
 def on_device(state, neighbour_map, layer_lists, forces, positions, route, element_slot):
     count = lax.axis_size("sfc")
-    inside = [(d, d ^ 1) for d in range(count)]
-    across = [(d, (d + 1) % count if d % 2 else (d - 1) % count) for d in range(count)]
-    par = (lax.axis_index("sfc") & 1).astype(jnp.int32).reshape(1)
-    pack, u, first, second, inv = entry_call(
-        par,
+    forward = [(d, (d + 1) % count) for d in range(count)]
+    backward = [(target, source) for source, target in forward]
+    pack, u, up, down, inv, order = entry_call(
         route.reshape(1, -1),
         element_slot.reshape(1, -1),
         forces,
@@ -594,12 +616,12 @@
         layer_lists,
         state.reshape(VARS * 16, 4, -1),
     )
-    second = lax.ppermute(second, "sfc", across)
-    first = lax.ppermute(first, "sfc", inside)
+    before = lax.ppermute(up, "sfc", forward)
+    after = lax.ppermute(down, "sfc", backward)
     pts = lax.all_to_all(pack, "sfc", split_axis=0, concat_axis=0, tiled=True)
-    base = state_call(par, u, first, second)
-    tail = slice(2 * COLS * 8, None)
-    out = source_call(par, pts, inv, first[tail], second[tail], base)
+    base = state_call(u, before, after)
+    table = slice(2 * COLS * 8, None)
+    out = source_call(pts, inv, before[table], after[table], base, order)
     return out.reshape(state.shape)
 
 

time: 32.3 us -> 31.5 us (0.975)
  starting transfers between devices: 13.8 us -> 13.3 us
    all_to_all x1, starting transfers between devices: 11 us -> 10.6 us  [on_device(): pts = lax.all_to_all(pack, 'sfc', split_axis=0, concat_axis=0, tiled=True)]
where the time goes in v2:
time: 31.5 us; the launch traced here: 31.3 us
  starting transfers between devices  13.3 us (42%)
  Pallas kernels  11.6 us (37%)
  waiting for transfers between devices  6.41 us (20%)
    all_to_all x1, starting transfers between devices, on_device(): pts = lax.all_to_all(pack, 'sfc', split_axis=0, concat_axis=0, tiled=True)  10.6 us
    all_to_all x1, waiting for transfers between devices, on_device(): pts = lax.all_to_all(pack, 'sfc', split_axis=0, concat_axis=0, tiled=True)  6.41 us
    pallas_call x1, Pallas kernels, source_call(): call(source_kernel, jax.ShapeDtypeStruct((VARS * 16, 4, 512), F32), [pltp...  4.61 us
    pallas_call x1, Pallas kernels, state_call(): call(state_kernel, tile_array(TILES), [cols, cols, cols, cols, pltpu.VMEM...  3.52 us
    pallas_call x1, Pallas kernels, entry_call(): call(entry_kernel, (jax.ShapeDtypeStruct((256, 128), F32), tile_array(TIL...  3.43 us
    ppermute x1, starting transfers between devices, on_device(): before = lax.ppermute(up, 'sfc', forward)  2.67 us
  transfers between devices with their start and end apart: 3, of which 1 were waited for; matrix products, arithmetic and copies ran while one was open for 0% of the time, Pallas kernels for 11%

profile of v2, /device:TPU:1, one launch (start us, length us, event | category | flops | bytes accessed | tf_op | source)
XLA Modules:
  0.0 31.3 jit_solution(4159798818153345431)
XLA Ops:
  0.0 3.4 %shard_map.64 = (f32[256,128]{1,0:T(8,128)}, f32[1280,128]{1,0:T(8,128)S(1)}, f32[648,128]{1,0:T(8,128)S(1)}, f32[648,128]{1,0:T(8,128)S(1)}, f32[8,128]{1,0:T(8,128)S(1)}, /*index=5*/bf16[512,512]{1,0:T(8,128)(2,1)S(1)}) custom-call(s32[1,512]{1,0:T(1,128)} %bitcast.8, s32[1,512]{1,0:T(1,128)} %bitcast.9, f32[5,512]{1,0:T(8,128)} %forces_hbm.1, ...), custom_call_target="tpu_custom_call" | custom-call | tf_op jit(solution)/shard_map/pallas_call | solution.py:550
  3.4 2.7 %collective-permute-start = (f32[648,128]{1,0:T(8,128)S(1)}, f32[648,128]{1,0:T(8,128)S(1)}, u32[]{:S(2)}, u32[]{:S(2)}) collective-permute-start(f32[648,128]{1,0:T(8,128)S(1)} %get-tuple-element.13), channel_id=1, source_target_pairs={{0,1},{1,2},{2,3},{3,4},{4,5},{5,6},{6,7},{7,8},{8,9},{9,10},{10,1... | collective-permute-start | bytes 995336 | tf_op jit(solution)/shard_map/ppermute | solution.py:619
  6.1 0.0 collective-permute-start.1
  6.1 10.6 %all-to-all-start = ((f32[128,2,128]{2,1,0:T(2,128)}), f32[128,2,128]{2,1,0:T(2,128)S(1)}, u32[]{:S(2)}, u32[]{:S(2)}) async-start(f32[128,2,128]{2,1,0:T(2,128)} %bitcast.3), calls=%async_computation | async-start | bytes 262144 | tf_op jit(solution)/shard_map/all_to_all | solution.py:621
  16.8 0.0 collective-permute-done.before_ref
  16.8 0.0 collective-permute-done.1.after_ref
  16.8 3.5 %shard_map.65.base_ref = f32[1280,128]{1,0:T(8,128)S(1)} custom-call(f32[1280,128]{1,0:T(8,128)S(1)} %get-tuple-element.15.u_ref, f32[648,128]{1,0:T(8,128)S(1)} %collective-permute-done.before_ref, f32[648,128]{1,0:T(8,128)S(1)} %collective-permute-done.1.after_ref), custom_call_target="tpu_custom_call" | custom-call | tf_op jit(solution)/shard_map/pallas_call | solution.py:571
  20.3 6.4 %all-to-all-done = f32[128,2,128]{2,1,0:T(2,128)S(1)} async-done(((f32[128,2,128]{2,1,0:T(2,128)}), f32[128,2,128]{2,1,0:T(2,128)S(1)}, u32[]{:S(2)}, u32[]{:S(2)}) %all-to-all-start) | async-done | bytes 131104 | tf_op jit(solution)/shard_map/all_to_all | solution.py:621
  26.7 4.6 %shard_map.66 = f32[80,4,512]{2,1,0:T(4,128)} custom-call(f32[256,128]{1,0:T(8,128)S(1)} %bitcast.6, f32[8,128]{1,0:T(8,128)S(1)} %get-tuple-element.12.inv_ref, f32[8,128]{1,0:T(8,128)S(1)} %slice.8.before_ref, f32[8,128]{1,0:T(8,128)S(1)} %slice.9.after_ref, f32[1280,128]{1,0:T(8,128)S(1)} %shard_map.65.base_ref, bf16[512,512]{1,0:T(8,128)(2,1)S(1)} %get-tuple-element.16.order), custom_call_target="tpu_custom_call" | custom-call | tf_op jit(solution)/shard_map/pallas_call | solution.py:582
  (2 shorter events, 0.0 us)
Async XLA Ops:
  3.4 13.3 %collective-permute-start = (f32[648,128]{1,0:T(8,128)S(1)}, f32[648,128]{1,0:T(8,128)S(1)}, u32[]{:S(2)}, u32[]{:S(2)}) collective-permute-start(f32[648,128]{1,0:T(8,128)S(1)} %get-tuple-element.13), channel_id=1, source_target_pairs={{0,1},{1,2},{2,3},{3,4},{4,5},{5,6},{6,7},{7,8},{8,9},{9,10},{10,1... | collective-permute-start | bytes 995336 | tf_op jit(solution)/shard_map/ppermute | solution.py:619
  6.1 10.7 %collective-permute-start.1 = (f32[648,128]{1,0:T(8,128)S(1)}, f32[648,128]{1,0:T(8,128)S(1)}, u32[]{:S(2)}, u32[]{:S(2)}) collective-permute-start(f32[648,128]{1,0:T(8,128)S(1)} %get-tuple-element.14), channel_id=1, source_target_pairs={{1,0},{2,1},{3,2},{4,3},{5,4},{6,5},{7,6},{8,7},{9,8},{10,9},{11,1... | collective-permute-start | bytes 995336 | tf_op jit(solution)/shard_map/ppermute | solution.py:620
  6.1 20.6 %all-to-all-start = ((f32[128,2,128]{2,1,0:T(2,128)}), f32[128,2,128]{2,1,0:T(2,128)S(1)}, u32[]{:S(2)}, u32[]{:S(2)}) async-start(f32[128,2,128]{2,1,0:T(2,128)} %bitcast.3), calls=%async_computation | async-start | bytes 262144 | tf_op jit(solution)/shard_map/all_to_all | solution.py:621

commit v3 on v2

--- a/solution.py
+++ b/solution.py
@@ -177,34 +177,39 @@
     mats[2][:, :4] += ident * np.eye(4)
     coefs = y_coefs(mk, mats[1])
 
-    def per_variable(v):
+    def in_layer(v):
         col = v * 8
-        for c in range(8):
-            u = [src[rows8((col + c) * 4 + k), :] for k in range(4)]
-            new = z_line(u, hu[rows8(col + c), :], hg[rows8(col + c), :], mk, mats[2])
+        for jj in range(2):
             for k in range(4):
-                dst[rows8((col + c) * 4 + k), :] = new[k]
+                at = [rows8((col + 2 * i + jj) * 4 + k) for i in range(4)]
+                new = x_line([src[a, :] for a in at], mk, mats[0])
+                for i in range(4):
+                    dst[at[i], :] = new[i]
         for i in range(4):
             for k in range(4):
                 at = [rows8((col + 2 * i + jj) * 4 + k) for jj in range(2)]
                 new = y_line(src[at[0], :], src[at[1], :], mk, coefs)
                 for jj in range(2):
                     dst[at[jj], :] += new[jj]
-        for jj in range(2):
+
+    def across(v):
+        col = v * 8
+        for c in range(8):
+            at = [rows8((col + c) * 4 + k) for k in range(4)]
+            u = [src[a, :] for a in at]
+            new = z_line(u, hu[rows8(col + c), :], hg[rows8(col + c), :], mk, mats[2])
             for k in range(4):
-                at = [rows8((col + 2 * i + jj) * 4 + k) for i in range(4)]
-                new = x_line([src[a, :] for a in at], mk, mats[0])
-                for i in range(4):
-                    dst[at[i], :] += new[i]
-
-    return per_variable
+                dst[at[k], :] += new[k]
+
+    return in_layer, across
 
 
 def apply_operator(*args):
-    one = operator_of(*args)
+    in_layer, across = operator_of(*args)
 
     def body(v, carry):
-        one(v)
+        in_layer(v)
+        across(v)
         return carry
 
     lax.fori_loop(0, VARS, body, 0)
@@ -236,9 +241,14 @@
 
 
 def fill_order(rows, order):
-    ids = lax.broadcasted_iota(jnp.int32, (512, 128), 0)
-    for t in range(4):
-        order[:, t * 128 : t * 128 + 128] = jnp.where(ids == rows[t], 1.0, 0.0).astype(BF16)
+    ids = lax.broadcasted_iota(jnp.int32, (16, 128), 0)
+    one, none = jnp.ones((16, 128), BF16), jnp.zeros((16, 128), BF16)
+    rows = [jnp.broadcast_to(row, (16, 128)).astype(jnp.int16) for row in rows]
+    for first in range(0, 512, 16):
+        here = (ids + first).astype(jnp.int16)
+        for t in range(4):
+            found = jnp.where(here == rows[t], one, none)
+            order[first : first + 16, t * 128 : t * 128 + 128] = found
 
 
 def pack_points(route, payload, pack_ref):
@@ -246,25 +256,27 @@
     lane = lax.broadcasted_iota(jnp.int32, (128, 128), 1)
     slot = lax.broadcasted_iota(jnp.int32, (8, 128), 0).astype(F32)
     to_device = [jnp.where(dest == route[:, t * 128 : t * 128 + 128], 1.0, 0.0) for t in range(4)]
-    stacked = jnp.concatenate(to_device, axis=0).astype(BF16)
+    narrow = [x.astype(BF16) for x in to_device]
     before = jnp.where(dest < lane, 1.0, 0.0).astype(BF16)
-    inside = jnp.dot(stacked, before, preferred_element_type=F32)
-    totals = jnp.dot(stacked, jnp.ones((128, 128), BF16), preferred_element_type=F32)
-    base = jnp.zeros((128, 128), F32)
-    out = jnp.zeros((128, 128), F32)
+    steps = jnp.concatenate([before, jnp.ones((128, 128), BF16)], axis=1)
+    counts = jnp.dot(jnp.concatenate(narrow, axis=0), steps, preferred_element_type=F32)
+    base = None
+    parts = [[], [], []]
     for t in range(4):
         here = slice(t * 128, t * 128 + 128)
-        count = inside[here] + base
-        base = base + totals[here]
+        count = counts[here, :128] if base is None else counts[here, :128] + base
+        base = counts[here, 128:] if base is None else base + counts[here, 128:]
         within = jnp.sum(count * to_device[t], axis=0, keepdims=True)
         chosen = slot == within
         rows = [jnp.where(chosen, p[:, here], 0.0) for p in payload]
-        rows.append(jnp.zeros((128 - GROUP, 128), F32))
+        rows.append(jnp.zeros((8, 128), F32))
         rest = jnp.concatenate(rows, axis=0)
-        for _ in range(3):
-            part = rest.astype(BF16)
-            rest = rest - part.astype(F32)
-            out = out + nt_dot(stacked[here], part)
+        for part in parts:
+            part.append(rest.astype(BF16))
+            rest = rest - part[-1].astype(F32)
+    terms = jnp.concatenate([jnp.concatenate(part, axis=1) for part in parts], axis=1)
+    terms = jnp.concatenate([terms, jnp.zeros((128 - GROUP - 8, 1536), BF16)], axis=0)
+    out = nt_dot(jnp.concatenate(narrow * 3, axis=1), terms)
     low = pltpu.roll(pltpu.roll(out, 1, 0), GROUP, 1)
     up = pltpu.roll(pltpu.roll(out, 127, 0), 2 * GROUP - 128, 1)
     pack_ref[pl.ds(0, 128, stride=2), :] = jnp.where(lane < GROUP, out, low)
@@ -275,7 +287,7 @@
     mat = TIME_STEP * LINES[2]
     sides = ((3, 2, UM, GM, up_ref), (0, -2, UP, GP, down_ref))
 
-    def per_variable(v, carry):
+    def per_variable(v):
         for c in range(8):
             col = v * 8 + c
             u = [u_ref[rows8(col * 4 + k), :] for k in range(4)]
@@ -290,9 +302,9 @@
                     a = rolled(a, -shift)
                     tile = jnp.where(mk.l0, a, b) if node == 3 else jnp.where(mk.l0, b, a)
                     goal[rows8(part * COLS + col), :] = tile
-        return carry
-
-    lax.fori_loop(0, VARS, per_variable, 0)
+
+    for v in range(VARS):
+        per_variable(v)
 
 
 def entry_kernel(
@@ -415,22 +427,14 @@
     return found.astype(jnp.int32)
 
 
-def fill_hots(hots, places):
+def fill_hot(hot, place):
     ids = lax.broadcasted_iota(jnp.int32, (16, 128), 0)
-    places = [[jnp.broadcast_to(p[c : c + 1, :], (16, 128)) for c in range(CAP)] for p in places]
-
-    def body(n, carry):
-        for hot, place in zip(hots, places):
-            count = hot.shape[0] // 256
-            for m in range(count):
-                first = (n * count + m) * 16
-                here = ids + first
-                for c in range(CAP):
-                    at = pl.ds(pl.multiple_of(first, 16), 16)
-                    hot[at, c * 128 : c * 128 + 128] = jnp.where(here == place[c], 1.0, 0.0).astype(BF16)
-        return carry
-
-    lax.fori_loop(0, 16, body, 0)
+    one, none = jnp.ones((16, 128), BF16), jnp.zeros((16, 128), BF16)
+    rows = [jnp.broadcast_to(place[c : c + 1, :], (16, 128)).astype(jnp.int16) for c in range(CAP)]
+    for first in range(0, hot.shape[0], 16):
+        here = (ids + first).astype(jnp.int16)
+        for c in range(CAP):
+            hot[first : first + 16, c * 128 : c * 128 + 128] = jnp.where(here == rows[c], one, none)
 
 
 def fill_terms(matrix, columns, nodes, strength, grid, group, first, count):
@@ -472,40 +476,44 @@
     field = [
         [data[g * GROUP + f * 8 : g * GROUP + f * 8 + 8] for f in range(FIELDS)] for g in range(3)
     ]
-    fill_hots(
-        (hot_low, hot_up, hot),
-        (
-            place_of(field[1][8], before_ref, 0) - 256,
-            place_of(field[2][8], after_ref, 0),
-            place_of(field[0][8], inv_ref, 0),
-        ),
-    )
-    traces = []
-    for group, node, matrix, goal in ((1, 3, lhs_low, hot_low), (2, 0, lhs_up, hot_up)):
-        fill_terms(matrix, *trace_terms(field[group], node), strength, grid, group, 0, 10)
-        traces.append(both(nt_dot(matrix[...], goal[...])))
     bx, by, bz = [line_basis(field[0][5 + d]) for d in range(3)]
     columns = [field[0][v] * bx[i] for v in range(VARS) for i in range(4)]
     nodes = [by[j] * bz[k] for j in NODE_ROWS for k in range(4)]
-    vals = []
-    for first, count in SPANS:
+    vals, traces, copies = {}, {}, []
+    in_layer, across = operator_of(
+        s_ref, new_ref, su, sg, mk, 0.5 * TIME_STEP * TIME_STEP, TIME_STEP
+    )
+
+    def gather(n):
+        first, count = SPANS[n]
         fill_terms(lhs, columns, nodes, strength, grid, 0, first * 4, count * 4)
-        vals.append(both(nt_dot(lhs[first * 128 : (first + count) * 128, :], hot[...])))
-    for part, goal in ((0, su), (1, sg)):
-        for v in range(VARS):
-            for h in range(2):
-                at = (part * VARS + v) * 16 + h * 8
-                for t in range(4):
-                    tile = traces[t // 2][at : at + 8, (t % 2) * 128 : (t % 2) * 128 + 128]
-                    goal[pl.ds(v * 64 + h * 4 + t, 8, stride=8), :] = tile
-
-    one = operator_of(s_ref, new_ref, su, sg, mk, 0.5 * TIME_STEP * TIME_STEP, TIME_STEP)
-    for (first, count), val in zip(SPANS, vals):
-        spread(val, s_ref, first * 4)
+        vals[n] = both(nt_dot(lhs[first * 128 : (first + count) * 128, :], hot[...]))
+
+    def gather_traces(side):
+        matrix, goal = ((lhs_low, hot_low), (lhs_up, hot_up))[side]
+        table, shift = ((before_ref, 256), (after_ref, 0))[side]
+        fill_hot(goal, place_of(field[1 + side][8], table, 0) - shift)
+        fill_terms(matrix, *trace_terms(field[1 + side], 3 - 3 * side), strength, grid, 1 + side, 0, 10)
+        traces[side] = both(nt_dot(matrix[...], goal[...]))
+
+    def spread_traces():
+        for part, goal in ((0, su), (1, sg)):
+            for v in range(VARS):
+                for h in range(2):
+                    at = (part * VARS + v) * 16 + h * 8
+                    for t in range(4):
+                        tile = traces[t // 2][at : at + 8, (t % 2) * 128 : (t % 2) * 128 + 128]
+                        goal[pl.ds(v * 64 + h * 4 + t, 8, stride=8), :] = tile
+
+    def advance(n, step):
+        first, count = SPANS[n]
+        if step is in_layer:
+            spread(vals[n], s_ref, first * 4)
         for v in range(first, first + count):
-            one(v)
-    copies = []
-    for n, (first, count) in enumerate(SPANS):
+            step(v)
+
+    def put_back(n):
+        first, count = SPANS[n]
         for vi in range(first * 4, (first + count) * 4):
             at = (first * 4 + vi) * 16
             for t in range(4):
@@ -523,6 +531,19 @@
         part = pl.ds(first * 16, count * 16)
         copies.append(pltpu.make_async_copy(out_ref.at[part], out_hbm.at[part], sems.at[n]))
         copies[-1].start()
+
+    fill_hot(hot, place_of(field[0][8], inv_ref, 0))
+    gather(0)
+    gather_traces(0)
+    gather_traces(1)
+    gather(1)
+    advance(0, in_layer)
+    spread_traces()
+    advance(0, across)
+    advance(1, in_layer)
+    put_back(0)
+    advance(1, across)
+    put_back(1)
     for copy in copies:
         copy.wait()
 

time: 31.5 us -> 30.1 us (0.956)
  Pallas kernels: 11.6 us -> 10.1 us
    pallas_call x1, Pallas kernels: 3.43 us -> 2.36 us  [entry_call(): call(entry_kernel, (jax.ShapeDtypeStruct((256, 128), F32), tile_array(TIL...]
    pallas_call x1, Pallas kernels: 4.61 us -> 4.29 us  [source_call(): call(source_kernel, jax.ShapeDtypeStruct((VARS * 16, 4, 512), F32), [pltp...]
  transfers between devices with their start and end apart: 3 -> 3, of which waited for: 1 -> 1; matrix products, arithmetic and copies ran while one was open for 0% -> 0% of each run, Pallas kernels for 11% -> 12%
where the time goes in v3:
time: 30.1 us; the launch traced here: 30 us
  starting transfers between devices  13.3 us (44%)
  Pallas kernels  10.1 us (34%)
  waiting for transfers between devices  6.45 us (21%)
    all_to_all x1, starting transfers between devices, on_device(): pts = lax.all_to_all(pack, 'sfc', split_axis=0, concat_axis=0, tiled=True)  10.6 us
    all_to_all x1, waiting for transfers between devices, on_device(): pts = lax.all_to_all(pack, 'sfc', split_axis=0, concat_axis=0, tiled=True)  6.44 us
    pallas_call x1, Pallas kernels, source_call(): call(source_kernel, jax.ShapeDtypeStruct((VARS * 16, 4, 512), F32), [pltp...  4.29 us
    pallas_call x1, Pallas kernels, state_call(): call(state_kernel, tile_array(TILES), [cols, cols, cols, cols, pltpu.VMEM...  3.49 us
    ppermute x1, starting transfers between devices, on_device(): before = lax.ppermute(up, 'sfc', forward)  2.67 us
    pallas_call x1, Pallas kernels, entry_call(): call(entry_kernel, (jax.ShapeDtypeStruct((256, 128), F32), tile_array(TIL...  2.36 us
  transfers between devices with their start and end apart: 3, of which 1 were waited for; matrix products, arithmetic and copies ran while one was open for 0% of the time, Pallas kernels for 12%

profile of v3, /device:TPU:1, one launch (start us, length us, event | category | flops | bytes accessed | tf_op | source)
XLA Modules:
  0.0 30.0 jit_solution(6058095307567018655)
XLA Ops:
  0.0 2.4 %shard_map.64 = (f32[256,128]{1,0:T(8,128)}, f32[1280,128]{1,0:T(8,128)S(1)}, f32[648,128]{1,0:T(8,128)S(1)}, f32[648,128]{1,0:T(8,128)S(1)}, f32[8,128]{1,0:T(8,128)S(1)}, /*index=5*/bf16[512,512]{1,0:T(8,128)(2,1)S(1)}) custom-call(s32[1,512]{1,0:T(1,128)} %bitcast.8, s32[1,512]{1,0:T(1,128)} %bitcast.9, f32[5,512]{1,0:T(8,128)} %forces_hbm.1, ...), custom_call_target="tpu_custom_call" | custom-call | tf_op jit(solution)/shard_map/pallas_call | solution.py:571
  2.4 2.7 %collective-permute-start = (f32[648,128]{1,0:T(8,128)S(1)}, f32[648,128]{1,0:T(8,128)S(1)}, u32[]{:S(2)}, u32[]{:S(2)}) collective-permute-start(f32[648,128]{1,0:T(8,128)S(1)} %get-tuple-element.13), channel_id=1, source_target_pairs={{0,1},{1,2},{2,3},{3,4},{4,5},{5,6},{6,7},{7,8},{8,9},{9,10},{10,1... | collective-permute-start | bytes 995336 | tf_op jit(solution)/shard_map/ppermute | solution.py:640
  5.0 0.0 collective-permute-start.1
  5.0 10.6 %all-to-all-start = ((f32[128,2,128]{2,1,0:T(2,128)}), f32[128,2,128]{2,1,0:T(2,128)S(1)}, u32[]{:S(2)}, u32[]{:S(2)}) async-start(f32[128,2,128]{2,1,0:T(2,128)} %bitcast.3), calls=%async_computation | async-start | bytes 262144 | tf_op jit(solution)/shard_map/all_to_all | solution.py:642
  15.7 0.0 collective-permute-done.before_ref
  15.7 0.0 collective-permute-done.1.after_ref
  15.7 3.5 %shard_map.65.base_ref = f32[1280,128]{1,0:T(8,128)S(1)} custom-call(f32[1280,128]{1,0:T(8,128)S(1)} %get-tuple-element.15.u_ref, f32[648,128]{1,0:T(8,128)S(1)} %collective-permute-done.before_ref, f32[648,128]{1,0:T(8,128)S(1)} %collective-permute-done.1.after_ref), custom_call_target="tpu_custom_call" | custom-call | tf_op jit(solution)/shard_map/pallas_call | solution.py:592
  19.2 6.4 %all-to-all-done = f32[128,2,128]{2,1,0:T(2,128)S(1)} async-done(((f32[128,2,128]{2,1,0:T(2,128)}), f32[128,2,128]{2,1,0:T(2,128)S(1)}, u32[]{:S(2)}, u32[]{:S(2)}) %all-to-all-start) | async-done | bytes 131104 | tf_op jit(solution)/shard_map/all_to_all | solution.py:642
  25.7 4.3 %shard_map.66 = f32[80,4,512]{2,1,0:T(4,128)} custom-call(f32[256,128]{1,0:T(8,128)S(1)} %bitcast.6, f32[8,128]{1,0:T(8,128)S(1)} %get-tuple-element.12.inv_ref, f32[8,128]{1,0:T(8,128)S(1)} %slice.8.before_ref, f32[8,128]{1,0:T(8,128)S(1)} %slice.9.after_ref, f32[1280,128]{1,0:T(8,128)S(1)} %shard_map.65.base_ref, bf16[512,512]{1,0:T(8,128)(2,1)S(1)} %get-tuple-element.16.order), custom_call_target="tpu_custom_call" | custom-call | tf_op jit(solution)/shard_map/pallas_call | solution.py:603
  (2 shorter events, 0.0 us)
Async XLA Ops:
  2.4 13.3 %collective-permute-start = (f32[648,128]{1,0:T(8,128)S(1)}, f32[648,128]{1,0:T(8,128)S(1)}, u32[]{:S(2)}, u32[]{:S(2)}) collective-permute-start(f32[648,128]{1,0:T(8,128)S(1)} %get-tuple-element.13), channel_id=1, source_target_pairs={{0,1},{1,2},{2,3},{3,4},{4,5},{5,6},{6,7},{7,8},{8,9},{9,10},{10,1... | collective-permute-start | bytes 995336 | tf_op jit(solution)/shard_map/ppermute | solution.py:640
  5.0 10.7 %collective-permute-start.1 = (f32[648,128]{1,0:T(8,128)S(1)}, f32[648,128]{1,0:T(8,128)S(1)}, u32[]{:S(2)}, u32[]{:S(2)}) collective-permute-start(f32[648,128]{1,0:T(8,128)S(1)} %get-tuple-element.14), channel_id=1, source_target_pairs={{1,0},{2,1},{3,2},{4,3},{5,4},{6,5},{7,6},{8,7},{9,8},{10,9},{11,1... | collective-permute-start | bytes 995336 | tf_op jit(solution)/shard_map/ppermute | solution.py:641
  5.0 20.6 %all-to-all-start = ((f32[128,2,128]{2,1,0:T(2,128)}), f32[128,2,128]{2,1,0:T(2,128)S(1)}, u32[]{:S(2)}, u32[]{:S(2)}) async-start(f32[128,2,128]{2,1,0:T(2,128)} %bitcast.3), calls=%async_computation | async-start | bytes 262144 | tf_op jit(solution)/shard_map/all_to_all | solution.py:642

commit v4 on v3

--- a/solution.py
+++ b/solution.py
@@ -21,6 +21,7 @@
 GROUP = FIELDS * CAP
 COLS = VARS * 4 * 2
 TILES = COLS * 4
+HALO_TILES = COLS * 3
 VMEM_LIMIT = 24 * 1024 * 1024
 F32 = jnp.float32
 BF16 = jnp.bfloat16
@@ -104,15 +105,20 @@
         self.y_wrap = (self.h0 & (lane < 16)) | (~self.h0 & (lane >= 112))
         self.sign = jnp.where(self.h0, 1.0, -1.0).astype(F32)
 
+    def by_layer(self, low, high):
+        return jnp.where(self.l0, float(low), float(high)).astype(F32)
+
     def by_half(self, low, high):
         if low == high:
             return float(low)
         return jnp.where(self.h0, float(low), float(high)).astype(F32)
 
 
-def rows8(index):
+def rows8(index, pitch=8):
     if isinstance(index, int):
-        return slice(index * 8, index * 8 + 8)
+        return slice(index * pitch, index * pitch + 8)
+    if pitch != 8:
+        return pl.ds(index * pitch, 8)
     return pl.ds(pl.multiple_of(index * 8, 8), 8)
 
 
@@ -172,40 +178,48 @@
     return [combine((mat[a, c], terms[c]) for c in range(8)) for a in range(4)]
 
 
-def operator_of(src, dst, hu, hg, mk, scale, ident):
+def operator_of(src, dst, hu, hg, mk, scale, ident, base=None, pitches=(8, 8)):
     mats = [scale * m for m in LINES]
     mats[2][:, :4] += ident * np.eye(4)
     coefs = y_coefs(mk, mats[1])
+
+    def read(index):
+        return src[rows8(index, pitches[0]), :]
+
+    def at_goal(index):
+        return rows8(index, pitches[1])
 
     def in_layer(v):
         col = v * 8
         for jj in range(2):
             for k in range(4):
-                at = [rows8((col + 2 * i + jj) * 4 + k) for i in range(4)]
-                new = x_line([src[a, :] for a in at], mk, mats[0])
+                at = [(col + 2 * i + jj) * 4 + k for i in range(4)]
+                new = x_line([read(n) for n in at], mk, mats[0])
                 for i in range(4):
-                    dst[at[i], :] = new[i]
+                    dst[at_goal(at[i]), :] = new[i]
         for i in range(4):
             for k in range(4):
-                at = [rows8((col + 2 * i + jj) * 4 + k) for jj in range(2)]
-                new = y_line(src[at[0], :], src[at[1], :], mk, coefs)
+                at = [(col + 2 * i + jj) * 4 + k for jj in range(2)]
+                new = y_line(read(at[0]), read(at[1]), mk, coefs)
                 for jj in range(2):
-                    dst[at[jj], :] += new[jj]
+                    dst[at_goal(at[jj]), :] += new[jj]
 
     def across(v):
         col = v * 8
         for c in range(8):
-            at = [rows8((col + c) * 4 + k) for k in range(4)]
-            u = [src[a, :] for a in at]
-            new = z_line(u, hu[rows8(col + c), :], hg[rows8(col + c), :], mk, mats[2])
+            at = [(col + c) * 4 + k for k in range(4)]
+            new = z_line(
+                [read(n) for n in at], hu[rows8(col + c), :], hg[rows8(col + c), :], mk, mats[2]
+            )
             for k in range(4):
-                dst[at[k], :] += new[k]
+                more = new[k] if base is None else new[k] + base[rows8(at[k]), :]
+                dst[at_goal(at[k]), :] += more
 
     return in_layer, across
 
 
-def apply_operator(*args):
-    in_layer, across = operator_of(*args)
+def apply_operator(*args, **options):
+    in_layer, across = operator_of(*args, **options)
 
     def body(v, carry):
         in_layer(v)
@@ -228,12 +242,15 @@
 NODE_ROWS = (0, 1, 3, 2)
 
 
-def spread(val, goal, first):
+PITCH = 12
+
+
+def spread(val, goal, first, pitch=8):
     for vi in range(val.shape[0] // 16):
         for h in range(2):
             for t in range(4):
                 tile = val[vi * 16 + h * 8 : vi * 16 + h * 8 + 8, t * 128 : t * 128 + 128]
-                goal[pl.ds((first + vi) * 64 + h * 4 + t, 8, stride=8), :] = tile
+                goal[pl.ds((first + vi) * 8 * pitch + h * 4 + t, 8, stride=pitch), :] = tile
 
 
 def nt_dot(a, b):
@@ -284,27 +301,15 @@
 
 
 def fill_halo(u_ref, up_ref, down_ref, mk):
-    mat = TIME_STEP * LINES[2]
-    sides = ((3, 2, UM, GM, up_ref), (0, -2, UP, GP, down_ref))
-
-    def per_variable(v):
-        for c in range(8):
-            col = v * 8 + c
-            u = [u_ref[rows8(col * 4 + k), :] for k in range(4)]
-            for node, shift, near, slope, goal in sides:
-                g = combine((SLOPE[node, b], u[b]) for b in range(4))
-                near_u, near_g = rolled(u[node], shift), rolled(g, shift)
-                for part, (row, a) in enumerate(((np.eye(4)[node], u[node]), (SLOPE[node], g))):
-                    b = combine(
-                        list(zip(row + row @ mat[:, :4], u))
-                        + [(row @ mat[:, near], near_u), (row @ mat[:, slope], near_g)]
-                    )
-                    a = rolled(a, -shift)
-                    tile = jnp.where(mk.l0, a, b) if node == 3 else jnp.where(mk.l0, b, a)
-                    goal[rows8(part * COLS + col), :] = tile
-
-    for v in range(VARS):
-        per_variable(v)
+    for col in range(COLS):
+        u = [u_ref[rows8(col * 4 + k), :] for k in range(4)]
+        g0 = combine((SLOPE[0, b], u[b]) for b in range(4))
+        g3 = combine((SLOPE[3, b], u[b]) for b in range(4))
+        ups = ((rolled(u[0], -2), u[1]), (rolled(u[2], -2), u[3]), (u[3], rolled(g3, 2)))
+        downs = ((u[0], rolled(u[1], 2)), (u[2], rolled(u[3], 2)), (rolled(u[0], -2), g0))
+        for part in range(3):
+            up_ref[rows8(part * COLS + col), :] = jnp.where(mk.l0, *ups[part])
+            down_ref[rows8(part * COLS + col), :] = jnp.where(mk.l0, *downs[part])
 
 
 def entry_kernel(
@@ -348,8 +353,8 @@
     inv = [inv[:, t * 128 : t * 128 + 128] for t in range(4)]
     inv = jnp.concatenate(inv + inv, axis=0)
     inv_ref[...] = inv
-    up_ref[2 * COLS * 8 :, :] = inv
-    down_ref[2 * COLS * 8 :, :] = inv
+    up_ref[HALO_TILES * 8 :, :] = inv
+    down_ref[HALO_TILES * 8 :, :] = inv
 
     fill_halo(u_ref, up_ref, down_ref, mk)
 
@@ -359,16 +364,35 @@
     mat = TIME_STEP * LINES[2]
     top, bottom = np.eye(4)[3], np.eye(4)[0]
 
-    def unpack(col, carry):
-        for part, (a, h) in enumerate(((au, hu), (ag, hg))):
-            low = before_ref[rows8(part * COLS + col), :]
-            high = after_ref[rows8(part * COLS + col), :]
-            a[rows8(col), :] = jnp.where(mk.l0, low, high)
-            h[rows8(col), :] = jnp.where(mk.l0, rolled(low, -2), rolled(high, 2))
+    def layered(row_low, row_high, near):
+        order = ((0, 1), (1, 0), (2, 3), (3, 2)) + (((UM, UP), (GM, GP)) if near else ())
+        return [mk.by_layer(row_low[low], row_high[high]) for low, high in order]
+
+    step = np.eye(4, 8) + mat
+    slopes = layered(SLOPE[3], SLOPE[0], False)
+    later = layered(step[3], step[0], True)
+    later_slopes = layered(SLOPE[3] @ step, SLOPE[0] @ step, True)
+
+    def unpack(v, carry):
+        for c in range(8):
+            col = v * 8 + c
+            low = [before_ref[rows8(part * COLS + col), :] for part in range(3)]
+            high = [after_ref[rows8(part * COLS + col), :] for part in range(3)]
+            tiles = []
+            for part in range(2):
+                tiles.append(jnp.where(mk.l0, low[part], high[part]))
+                tiles.append(jnp.where(mk.l0, rolled(low[part], -2), rolled(high[part], 2)))
+            tiles.append(jnp.where(mk.l0, low[2], rolled(high[2], 2)))
+            tiles.append(jnp.where(mk.l0, rolled(low[2], -2), high[2]))
+            at = rows8(col)
+            au[at, :] = jnp.where(mk.l0, tiles[3], tiles[1])
+            ag[at, :] = combine(zip(slopes, tiles))
+            hu[at, :] = combine(zip(later, tiles))
+            hg[at, :] = combine(zip(later_slopes, tiles))
         return carry
 
-    lax.fori_loop(0, COLS, unpack, 0, unroll=8)
-    apply_operator(u_ref, m0, au, ag, mk, TIME_STEP, 1.0)
+    lax.fori_loop(0, VARS, unpack, 0)
+    apply_operator(u_ref, m0, au, ag, mk, TIME_STEP, 1.0, pitches=(8, 8))
 
     x_mat, coefs = TIME_STEP * LINES[0], y_coefs(mk, TIME_STEP * LINES[1])
 
@@ -463,6 +487,7 @@
 
 
 SPANS = ((0, 3), (3, 2))
+BACK = ((0, 3), (3, 2))
 
 
 def source_kernel(
@@ -481,7 +506,7 @@
     nodes = [by[j] * bz[k] for j in NODE_ROWS for k in range(4)]
     vals, traces, copies = {}, {}, []
     in_layer, across = operator_of(
-        s_ref, new_ref, su, sg, mk, 0.5 * TIME_STEP * TIME_STEP, TIME_STEP
+        s_ref, new_ref, su, sg, mk, 0.5 * TIME_STEP * TIME_STEP, TIME_STEP, base_ref, (PITCH, PITCH)
     )
 
     def gather(n):
@@ -508,7 +533,7 @@
     def advance(n, step):
         first, count = SPANS[n]
         if step is in_layer:
-            spread(vals[n], s_ref, first * 4)
+            spread(vals[n], s_ref, first * 4, PITCH)
         for v in range(first, first + count):
             step(v)
 
@@ -517,8 +542,8 @@
         for vi in range(first * 4, (first + count) * 4):
             at = (first * 4 + vi) * 16
             for t in range(4):
-                rows = [pl.ds(vi * 64 + h * 4 + t, 8, stride=8) for h in range(2)]
-                x = jnp.concatenate([new_ref[r, :] + base_ref[r, :] for r in rows], axis=0)
+                rows = [pl.ds(vi * 8 * PITCH + h * 4 + t, 8, stride=PITCH) for h in range(2)]
+                x = jnp.concatenate([new_ref[r, :] for r in rows], axis=0)
                 hi, lo = split2(x)
                 lhs_out[at : at + 16, t * 128 : t * 128 + 128] = hi
                 at_lo = at + count * 64
@@ -573,8 +598,8 @@
         (
             jax.ShapeDtypeStruct((256, 128), F32),
             tile_array(TILES),
-            tile_array(2 * COLS + 1),
-            tile_array(2 * COLS + 1),
+            tile_array(HALO_TILES + 1),
+            tile_array(HALO_TILES + 1),
             tile_array(1),
             jax.ShapeDtypeStruct((512, 512), BF16),
         ),
@@ -599,7 +624,7 @@
 
 def source_call(pts, inv, before, after, base, order):
     cols = pltpu.VMEM((COLS * 8, 128), F32)
-    field = pltpu.VMEM((TILES * 8, 128), F32)
+    field = pltpu.VMEM((TILES * PITCH, 128), F32)
     return call(
         source_kernel,
         jax.ShapeDtypeStruct((VARS * 16, 4, 512), F32),
@@ -641,7 +666,7 @@
     after = lax.ppermute(down, "sfc", backward)
     pts = lax.all_to_all(pack, "sfc", split_axis=0, concat_axis=0, tiled=True)
     base = state_call(u, before, after)
-    table = slice(2 * COLS * 8, None)
+    table = slice(HALO_TILES * 8, None)
     out = source_call(pts, inv, before[table], after[table], base, order)
     return out.reshape(state.shape)
 

time: 30.1 us -> 29.8 us (0.990)
  no operation moved by 1% of the time
where the time goes in v4:
time: 29.8 us; the launch traced here: 29.6 us
  starting transfers between devices  13.3 us (45%)
  Pallas kernels  9.98 us (33%)
  waiting for transfers between devices  6.25 us (21%)
    all_to_all x1, starting transfers between devices, on_device(): pts = lax.all_to_all(pack, 'sfc', split_axis=0, concat_axis=0, tiled=True)  10.6 us
    all_to_all x1, waiting for transfers between devices, on_device(): pts = lax.all_to_all(pack, 'sfc', split_axis=0, concat_axis=0, tiled=True)  6.25 us
    pallas_call x1, Pallas kernels, source_call(): call(source_kernel, jax.ShapeDtypeStruct((VARS * 16, 4, 512), F32), [pltp...  4.1 us
    pallas_call x1, Pallas kernels, state_call(): call(state_kernel, tile_array(TILES), [cols, cols, cols, cols, pltpu.VMEM...  3.68 us
    ppermute x1, starting transfers between devices, on_device(): before = lax.ppermute(up, 'sfc', forward)  2.67 us
    pallas_call x1, Pallas kernels, entry_call(): call(entry_kernel, (jax.ShapeDtypeStruct((256, 128), F32), tile_array(TIL...  2.2 us
  transfers between devices with their start and end apart: 3, of which 1 were waited for; matrix products, arithmetic and copies ran while one was open for 0% of the time, Pallas kernels for 12%

profile of v4, /device:TPU:1, one launch (start us, length us, event | category | flops | bytes accessed | tf_op | source)
XLA Modules:
  0.0 29.6 jit_solution(14040973164527992276)
XLA Ops:
  0.0 2.2 %shard_map.64 = (f32[256,128]{1,0:T(8,128)}, f32[1280,128]{1,0:T(8,128)S(1)}, f32[968,128]{1,0:T(8,128)S(1)}, f32[968,128]{1,0:T(8,128)S(1)}, f32[8,128]{1,0:T(8,128)S(1)}, /*index=5*/bf16[512,512]{1,0:T(8,128)(2,1)S(1)}) custom-call(s32[1,512]{1,0:T(1,128)} %bitcast.8, s32[1,512]{1,0:T(1,128)} %bitcast.9, f32[5,512]{1,0:T(8,128)} %forces_hbm.1, ...), custom_call_target="tpu_custom_call" | custom-call | tf_op jit(solution)/shard_map/pallas_call | solution.py:596
  2.2 2.7 %collective-permute-start = (f32[968,128]{1,0:T(8,128)S(1)}, f32[968,128]{1,0:T(8,128)S(1)}, u32[]{:S(2)}, u32[]{:S(2)}) collective-permute-start(f32[968,128]{1,0:T(8,128)S(1)} %get-tuple-element.13), channel_id=1, source_target_pairs={{0,1},{1,2},{2,3},{3,4},{4,5},{5,6},{6,7},{7,8},{8,9},{9,10},{10,1... | collective-permute-start | bytes 1486856 | tf_op jit(solution)/shard_map/ppermute | solution.py:665
  4.9 0.0 collective-permute-start.1
  4.9 10.6 %all-to-all-start = ((f32[128,2,128]{2,1,0:T(2,128)}), f32[128,2,128]{2,1,0:T(2,128)S(1)}, u32[]{:S(2)}, u32[]{:S(2)}) async-start(f32[128,2,128]{2,1,0:T(2,128)} %bitcast.3), calls=%async_computation | async-start | bytes 262144 | tf_op jit(solution)/shard_map/all_to_all | solution.py:667
  15.5 0.0 collective-permute-done.before_ref
  15.5 0.0 collective-permute-done.1.after_ref
  15.6 3.7 %shard_map.65.base_ref = f32[1280,128]{1,0:T(8,128)S(1)} custom-call(f32[1280,128]{1,0:T(8,128)S(1)} %get-tuple-element.15.u_ref, f32[968,128]{1,0:T(8,128)S(1)} %collective-permute-done.before_ref, f32[968,128]{1,0:T(8,128)S(1)} %collective-permute-done.1.after_ref), custom_call_target="tpu_custom_call" | custom-call | tf_op jit(solution)/shard_map/pallas_call | solution.py:617
  19.3 6.2 %all-to-all-done = f32[128,2,128]{2,1,0:T(2,128)S(1)} async-done(((f32[128,2,128]{2,1,0:T(2,128)}), f32[128,2,128]{2,1,0:T(2,128)S(1)}, u32[]{:S(2)}, u32[]{:S(2)}) %all-to-all-start) | async-done | bytes 131104 | tf_op jit(solution)/shard_map/all_to_all | solution.py:667
  25.5 4.1 %shard_map.66 = f32[80,4,512]{2,1,0:T(4,128)} custom-call(f32[256,128]{1,0:T(8,128)S(1)} %bitcast.6, f32[8,128]{1,0:T(8,128)S(1)} %get-tuple-element.12.inv_ref, f32[8,128]{1,0:T(8,128)S(1)} %slice.8.before_ref, f32[8,128]{1,0:T(8,128)S(1)} %slice.9.after_ref, f32[1280,128]{1,0:T(8,128)S(1)} %shard_map.65.base_ref, bf16[512,512]{1,0:T(8,128)(2,1)S(1)} %get-tuple-element.16.order), custom_call_target="tpu_custom_call" | custom-call | tf_op jit(solution)/shard_map/pallas_call | solution.py:628
  (2 shorter events, 0.0 us)
Async XLA Ops:
  2.2 13.3 %collective-permute-start = (f32[968,128]{1,0:T(8,128)S(1)}, f32[968,128]{1,0:T(8,128)S(1)}, u32[]{:S(2)}, u32[]{:S(2)}) collective-permute-start(f32[968,128]{1,0:T(8,128)S(1)} %get-tuple-element.13), channel_id=1, source_target_pairs={{0,1},{1,2},{2,3},{3,4},{4,5},{5,6},{6,7},{7,8},{8,9},{9,10},{10,1... | collective-permute-start | bytes 1486856 | tf_op jit(solution)/shard_map/ppermute | solution.py:665
  4.9 10.7 %collective-permute-start.1 = (f32[968,128]{1,0:T(8,128)S(1)}, f32[968,128]{1,0:T(8,128)S(1)}, u32[]{:S(2)}, u32[]{:S(2)}) collective-permute-start(f32[968,128]{1,0:T(8,128)S(1)} %get-tuple-element.14), channel_id=1, source_target_pairs={{1,0},{2,1},{3,2},{4,3},{5,4},{6,5},{7,6},{8,7},{9,8},{10,9},{11,1... | collective-permute-start | bytes 1486856 | tf_op jit(solution)/shard_map/ppermute | solution.py:666
  4.9 20.6 %all-to-all-start = ((f32[128,2,128]{2,1,0:T(2,128)}), f32[128,2,128]{2,1,0:T(2,128)S(1)}, u32[]{:S(2)}, u32[]{:S(2)}) async-start(f32[128,2,128]{2,1,0:T(2,128)} %bitcast.3), calls=%async_computation | async-start | bytes 262144 | tf_op jit(solution)/shard_map/all_to_all | solution.py:667

commit v5 on v4

--- a/solution.py
+++ b/solution.py
@@ -487,7 +487,7 @@
 
 
 SPANS = ((0, 3), (3, 2))
-BACK = ((0, 3), (3, 2))
+BACK = ((0, 3), (3, 1), (4, 1))
 
 
 def source_kernel(
@@ -538,7 +538,7 @@
             step(v)
 
     def put_back(n):
-        first, count = SPANS[n]
+        first, count = BACK[n]
         for vi in range(first * 4, (first + count) * 4):
             at = (first * 4 + vi) * 16
             for t in range(4):
@@ -569,6 +569,7 @@
     put_back(0)
     advance(1, across)
     put_back(1)
+    put_back(2)
     for copy in copies:
         copy.wait()
 
@@ -643,7 +644,7 @@
             field,
             pltpu.VMEM((640, 512), BF16),
             pltpu.VMEM((VARS * 16, 4, 512), F32),
-            pltpu.SemaphoreType.DMA((2,)),
+            pltpu.SemaphoreType.DMA((3,)),
         ],
         [VMEM] * 6,
         pltpu.HBM,

time: 29.8 us -> 29.7 us (level)
  no operation moved by 1% of the time
where the time goes in v5:
time: 29.7 us; the launch traced here: 29.6 us
  starting transfers between devices  13.3 us (45%)
  Pallas kernels  9.93 us (33%)
  waiting for transfers between devices  6.25 us (21%)
    all_to_all x1, starting transfers between devices, on_device(): pts = lax.all_to_all(pack, 'sfc', split_axis=0, concat_axis=0, tiled=True)  10.6 us
    all_to_all x1, waiting for transfers between devices, on_device(): pts = lax.all_to_all(pack, 'sfc', split_axis=0, concat_axis=0, tiled=True)  6.25 us
    pallas_call x1, Pallas kernels, source_call(): call(source_kernel, jax.ShapeDtypeStruct((VARS * 16, 4, 512), F32), [pltp...  4.05 us
    pallas_call x1, Pallas kernels, state_call(): call(state_kernel, tile_array(TILES), [cols, cols, cols, cols, pltpu.VMEM...  3.68 us
    ppermute x1, starting transfers between devices, on_device(): before = lax.ppermute(up, 'sfc', forward)  2.67 us
    pallas_call x1, Pallas kernels, entry_call(): call(entry_kernel, (jax.ShapeDtypeStruct((256, 128), F32), tile_array(TIL...  2.2 us
  transfers between devices with their start and end apart: 3, of which 1 were waited for; matrix products, arithmetic and copies ran while one was open for 0% of the time, Pallas kernels for 12%

profile of v5, /device:TPU:1, one launch (start us, length us, event | category | flops | bytes accessed | tf_op | source)
XLA Modules:
  0.0 29.6 jit_solution(5193162789197216884)
XLA Ops:
  0.0 2.2 %shard_map.64 = (f32[256,128]{1,0:T(8,128)}, f32[1280,128]{1,0:T(8,128)S(1)}, f32[968,128]{1,0:T(8,128)S(1)}, f32[968,128]{1,0:T(8,128)S(1)}, f32[8,128]{1,0:T(8,128)S(1)}, /*index=5*/bf16[512,512]{1,0:T(8,128)(2,1)S(1)}) custom-call(s32[1,512]{1,0:T(1,128)} %bitcast.8, s32[1,512]{1,0:T(1,128)} %bitcast.9, f32[5,512]{1,0:T(8,128)} %forces_hbm.1, ...), custom_call_target="tpu_custom_call" | custom-call | tf_op jit(solution)/shard_map/pallas_call | solution.py:597
  2.2 2.7 %collective-permute-start = (f32[968,128]{1,0:T(8,128)S(1)}, f32[968,128]{1,0:T(8,128)S(1)}, u32[]{:S(2)}, u32[]{:S(2)}) collective-permute-start(f32[968,128]{1,0:T(8,128)S(1)} %get-tuple-element.13), channel_id=1, source_target_pairs={{0,1},{1,2},{2,3},{3,4},{4,5},{5,6},{6,7},{7,8},{8,9},{9,10},{10,1... | collective-permute-start | bytes 1486856 | tf_op jit(solution)/shard_map/ppermute | solution.py:666
  4.9 0.0 collective-permute-start.1
  4.9 10.6 %all-to-all-start = ((f32[128,2,128]{2,1,0:T(2,128)}), f32[128,2,128]{2,1,0:T(2,128)S(1)}, u32[]{:S(2)}, u32[]{:S(2)}) async-start(f32[128,2,128]{2,1,0:T(2,128)} %bitcast.3), calls=%async_computation | async-start | bytes 262144 | tf_op jit(solution)/shard_map/all_to_all | solution.py:668
  15.5 0.0 collective-permute-done.before_ref
  15.5 0.0 collective-permute-done.1.after_ref
  15.6 3.7 %shard_map.65.base_ref = f32[1280,128]{1,0:T(8,128)S(1)} custom-call(f32[1280,128]{1,0:T(8,128)S(1)} %get-tuple-element.15.u_ref, f32[968,128]{1,0:T(8,128)S(1)} %collective-permute-done.before_ref, f32[968,128]{1,0:T(8,128)S(1)} %collective-permute-done.1.after_ref), custom_call_target="tpu_custom_call" | custom-call | tf_op jit(solution)/shard_map/pallas_call | solution.py:618
  19.3 6.2 %all-to-all-done = f32[128,2,128]{2,1,0:T(2,128)S(1)} async-done(((f32[128,2,128]{2,1,0:T(2,128)}), f32[128,2,128]{2,1,0:T(2,128)S(1)}, u32[]{:S(2)}, u32[]{:S(2)}) %all-to-all-start) | async-done | bytes 131104 | tf_op jit(solution)/shard_map/all_to_all | solution.py:668
  25.5 4.1 %shard_map.66 = f32[80,4,512]{2,1,0:T(4,128)} custom-call(f32[256,128]{1,0:T(8,128)S(1)} %bitcast.6, f32[8,128]{1,0:T(8,128)S(1)} %get-tuple-element.12.inv_ref, f32[8,128]{1,0:T(8,128)S(1)} %slice.8.before_ref, f32[8,128]{1,0:T(8,128)S(1)} %slice.9.after_ref, f32[1280,128]{1,0:T(8,128)S(1)} %shard_map.65.base_ref, bf16[512,512]{1,0:T(8,128)(2,1)S(1)} %get-tuple-element.16.order), custom_call_target="tpu_custom_call" | custom-call | tf_op jit(solution)/shard_map/pallas_call | solution.py:629
  (2 shorter events, 0.0 us)
Async XLA Ops:
  2.2 13.3 %collective-permute-start = (f32[968,128]{1,0:T(8,128)S(1)}, f32[968,128]{1,0:T(8,128)S(1)}, u32[]{:S(2)}, u32[]{:S(2)}) collective-permute-start(f32[968,128]{1,0:T(8,128)S(1)} %get-tuple-element.13), channel_id=1, source_target_pairs={{0,1},{1,2},{2,3},{3,4},{4,5},{5,6},{6,7},{7,8},{8,9},{9,10},{10,1... | collective-permute-start | bytes 1486856 | tf_op jit(solution)/shard_map/ppermute | solution.py:666
  4.9 10.7 %collective-permute-start.1 = (f32[968,128]{1,0:T(8,128)S(1)}, f32[968,128]{1,0:T(8,128)S(1)}, u32[]{:S(2)}, u32[]{:S(2)}) collective-permute-start(f32[968,128]{1,0:T(8,128)S(1)} %get-tuple-element.14), channel_id=1, source_target_pairs={{1,0},{2,1},{3,2},{4,3},{5,4},{6,5},{7,6},{8,7},{9,8},{10,9},{11,1... | collective-permute-start | bytes 1486856 | tf_op jit(solution)/shard_map/ppermute | solution.py:667
  4.9 20.6 %all-to-all-start = ((f32[128,2,128]{2,1,0:T(2,128)}), f32[128,2,128]{2,1,0:T(2,128)S(1)}, u32[]{:S(2)}, u32[]{:S(2)}) async-start(f32[128,2,128]{2,1,0:T(2,128)} %bitcast.3), calls=%async_computation | async-start | bytes 262144 | tf_op jit(solution)/shard_map/all_to_all | solution.py:668

commit v6 on v5

--- a/solution.py
+++ b/solution.py
@@ -461,7 +461,8 @@
             hot[first : first + 16, c * 128 : c * 128 + 128] = jnp.where(here == rows[c], one, none)
 
 
-def fill_terms(matrix, columns, nodes, strength, grid, group, first, count):
+def fill_terms(matrix, columns, nodes, strength, grid, group, first, count, split=None):
+    split = count if split is None else split
     if first == 0:
         for n, tile in enumerate(nodes):
             grid[group, n * 8 : n * 8 + 8, :] = tile
@@ -474,7 +475,8 @@
             hi, lo = split2(node_rows * strength[group, n * 8 + c : n * 8 + c + 1, :])
             at = (first + n) * 16
             matrix[at : at + 16, here] = hi
-            matrix[at + count * 16 : at + count * 16 + 16, here] = lo
+            if n - first < split:
+                matrix[at + count * 16 : at + count * 16 + 16, here] = lo
 
 
 def trace_terms(field, node):
@@ -518,8 +520,9 @@
         matrix, goal = ((lhs_low, hot_low), (lhs_up, hot_up))[side]
         table, shift = ((before_ref, 256), (after_ref, 0))[side]
         fill_hot(goal, place_of(field[1 + side][8], table, 0) - shift)
-        fill_terms(matrix, *trace_terms(field[1 + side], 3 - 3 * side), strength, grid, 1 + side, 0, 10)
-        traces[side] = both(nt_dot(matrix[...], goal[...]))
+        fill_terms(matrix, *trace_terms(field[1 + side], 3 - 3 * side), strength, grid, 1 + side, 0, 10, 5)
+        res = nt_dot(matrix[...], goal[...])
+        traces[side] = jnp.concatenate([res[:80] + res[160:], res[80:160]], axis=0)
 
     def spread_traces():
         for part, goal in ((0, su), (1, sg)):
@@ -634,8 +637,8 @@
             pltpu.VMEM((256, 1024), BF16),
             pltpu.VMEM((256, 1024), BF16),
             pltpu.VMEM((640, 1024), BF16),
-            pltpu.VMEM((320, 1024), BF16),
-            pltpu.VMEM((320, 1024), BF16),
+            pltpu.VMEM((240, 1024), BF16),
+            pltpu.VMEM((240, 1024), BF16),
             pltpu.VMEM((3, 128, 128), F32),
             pltpu.VMEM((3, 160, 128), F32),
             cols,

time: 29.7 us -> 29.6 us (level)
  no operation moved by 1% of the time
where the time goes in v6:
time: 29.6 us; the launch traced here: 29.5 us
  starting transfers between devices  13.3 us (45%)
  Pallas kernels  9.84 us (33%)
  waiting for transfers between devices  6.25 us (21%)
    all_to_all x1, starting transfers between devices, on_device(): pts = lax.all_to_all(pack, 'sfc', split_axis=0, concat_axis=0, tiled=True)  10.6 us
    all_to_all x1, waiting for transfers between devices, on_device(): pts = lax.all_to_all(pack, 'sfc', split_axis=0, concat_axis=0, tiled=True)  6.25 us
    pallas_call x1, Pallas kernels, source_call(): call(source_kernel, jax.ShapeDtypeStruct((VARS * 16, 4, 512), F32), [pltp...  3.96 us
    pallas_call x1, Pallas kernels, state_call(): call(state_kernel, tile_array(TILES), [cols, cols, cols, cols, pltpu.VMEM...  3.68 us
    ppermute x1, starting transfers between devices, on_device(): before = lax.ppermute(up, 'sfc', forward)  2.67 us
    pallas_call x1, Pallas kernels, entry_call(): call(entry_kernel, (jax.ShapeDtypeStruct((256, 128), F32), tile_array(TIL...  2.2 us
  transfers between devices with their start and end apart: 3, of which 1 were waited for; matrix products, arithmetic and copies ran while one was open for 0% of the time, Pallas kernels for 12%

profile of v6, /device:TPU:1, one launch (start us, length us, event | category | flops | bytes accessed | tf_op | source)
XLA Modules:
  0.0 29.5 jit_solution(10894271140120188399)
XLA Ops:
  0.0 2.2 %shard_map.64 = (f32[256,128]{1,0:T(8,128)}, f32[1280,128]{1,0:T(8,128)S(1)}, f32[968,128]{1,0:T(8,128)S(1)}, f32[968,128]{1,0:T(8,128)S(1)}, f32[8,128]{1,0:T(8,128)S(1)}, /*index=5*/bf16[512,512]{1,0:T(8,128)(2,1)S(1)}) custom-call(s32[1,512]{1,0:T(1,128)} %bitcast.8, s32[1,512]{1,0:T(1,128)} %bitcast.9, f32[5,512]{1,0:T(8,128)} %forces_hbm.1, ...), custom_call_target="tpu_custom_call" | custom-call | tf_op jit(solution)/shard_map/pallas_call | solution.py:600
  2.2 2.7 %collective-permute-start = (f32[968,128]{1,0:T(8,128)S(1)}, f32[968,128]{1,0:T(8,128)S(1)}, u32[]{:S(2)}, u32[]{:S(2)}) collective-permute-start(f32[968,128]{1,0:T(8,128)S(1)} %get-tuple-element.13), channel_id=1, source_target_pairs={{0,1},{1,2},{2,3},{3,4},{4,5},{5,6},{6,7},{7,8},{8,9},{9,10},{10,1... | collective-permute-start | bytes 1486856 | tf_op jit(solution)/shard_map/ppermute | solution.py:669
  4.9 0.0 collective-permute-start.1
  4.9 10.6 %all-to-all-start = ((f32[128,2,128]{2,1,0:T(2,128)}), f32[128,2,128]{2,1,0:T(2,128)S(1)}, u32[]{:S(2)}, u32[]{:S(2)}) async-start(f32[128,2,128]{2,1,0:T(2,128)} %bitcast.3), calls=%async_computation | async-start | bytes 262144 | tf_op jit(solution)/shard_map/all_to_all | solution.py:671
  15.5 0.0 collective-permute-done.before_ref
  15.5 0.0 collective-permute-done.1.after_ref
  15.6 3.7 %shard_map.65.base_ref = f32[1280,128]{1,0:T(8,128)S(1)} custom-call(f32[1280,128]{1,0:T(8,128)S(1)} %get-tuple-element.15.u_ref, f32[968,128]{1,0:T(8,128)S(1)} %collective-permute-done.before_ref, f32[968,128]{1,0:T(8,128)S(1)} %collective-permute-done.1.after_ref), custom_call_target="tpu_custom_call" | custom-call | tf_op jit(solution)/shard_map/pallas_call | solution.py:621
  19.3 6.2 %all-to-all-done = f32[128,2,128]{2,1,0:T(2,128)S(1)} async-done(((f32[128,2,128]{2,1,0:T(2,128)}), f32[128,2,128]{2,1,0:T(2,128)S(1)}, u32[]{:S(2)}, u32[]{:S(2)}) %all-to-all-start) | async-done | bytes 131104 | tf_op jit(solution)/shard_map/all_to_all | solution.py:671
  25.5 4.0 %shard_map.66 = f32[80,4,512]{2,1,0:T(4,128)} custom-call(f32[256,128]{1,0:T(8,128)S(1)} %bitcast.6, f32[8,128]{1,0:T(8,128)S(1)} %get-tuple-element.12.inv_ref, f32[8,128]{1,0:T(8,128)S(1)} %slice.8.before_ref, f32[8,128]{1,0:T(8,128)S(1)} %slice.9.after_ref, f32[1280,128]{1,0:T(8,128)S(1)} %shard_map.65.base_ref, bf16[512,512]{1,0:T(8,128)(2,1)S(1)} %get-tuple-element.16.order), custom_call_target="tpu_custom_call" | custom-call | tf_op jit(solution)/shard_map/pallas_call | solution.py:632
  (2 shorter events, 0.0 us)
Async XLA Ops:
  2.2 13.3 %collective-permute-start = (f32[968,128]{1,0:T(8,128)S(1)}, f32[968,128]{1,0:T(8,128)S(1)}, u32[]{:S(2)}, u32[]{:S(2)}) collective-permute-start(f32[968,128]{1,0:T(8,128)S(1)} %get-tuple-element.13), channel_id=1, source_target_pairs={{0,1},{1,2},{2,3},{3,4},{4,5},{5,6},{6,7},{7,8},{8,9},{9,10},{10,1... | collective-permute-start | bytes 1486856 | tf_op jit(solution)/shard_map/ppermute | solution.py:669
  4.9 10.7 %collective-permute-start.1 = (f32[968,128]{1,0:T(8,128)S(1)}, f32[968,128]{1,0:T(8,128)S(1)}, u32[]{:S(2)}, u32[]{:S(2)}) collective-permute-start(f32[968,128]{1,0:T(8,128)S(1)} %get-tuple-element.14), channel_id=1, source_target_pairs={{1,0},{2,1},{3,2},{4,3},{5,4},{6,5},{7,6},{8,7},{9,8},{10,9},{11,1... | collective-permute-start | bytes 1486856 | tf_op jit(solution)/shard_map/ppermute | solution.py:670
  4.9 20.6 %all-to-all-start = ((f32[128,2,128]{2,1,0:T(2,128)}), f32[128,2,128]{2,1,0:T(2,128)S(1)}, u32[]{:S(2)}, u32[]{:S(2)}) async-start(f32[128,2,128]{2,1,0:T(2,128)} %bitcast.3), calls=%async_computation | async-start | bytes 262144 | tf_op jit(solution)/shard_map/all_to_all | solution.py:671
